TPU v7x, 128 devices: a whole 4x4x4 slice. The times are simulated.
128 devices in a mesh: au: 32 (over y, z, core), ia: 4 (over x).
Axes of the slice: x: 4, y: 4, z: 4, core: 2. Of those that a mesh axis runs over, the one named last changes fastest.
Arguments:
- tile_values: bfloat16 [32768, 128, 128], P(('au', 'ia')), may hold values from -6 to 6
- tile_index: int32 [3, 32768], P(None, ('au', 'ia')), may hold values from 0 to 31, as said below
- tile_count: int32 [128], P(('au', 'ia')), may hold values from 32 to 256, as said below
- user_prev: float32 [64, 131072], P(None, 'au')
- item_prev: float32 [64, 16384], P(None, 'ia')
- day_prior: float32 [64, 32], replicated, may hold values from -6 to 6
Outputs:
- user_factor: float32 [64, 131072], P(None, 'au')
- item_factor: float32 [64, 16384], P(None, 'ia')
- day_factor: float32 [64, 32], replicated
Inputs may be any that keep to these rules, and one draw needn't show every extreme that they name: `tile_index`: row 0 is a user block among the 32 of the device's users, row 1 an item block among the 32 of its items, row 2 a day; slots at or past a device's count are ignored. `tile_count`: some device is full in every draw.
All inputs are finite; a program needn't handle non-finite values.
Results may differ from a plain program's by a relative error of at most 0.0016.
Values sent between devices are 32-bit elements; how exact they have to be, the bound alone decides.
A program may use at most 64 MiB of HBM per device.

v0:
```python
import math

import jax
import jax.numpy as jnp
from jax import lax
from jax.sharding import PartitionSpec as P

PASSES = 2


EPSILON = 1e-06
HIGHEST = lax.Precision.HIGHEST


def pick_blocks(rows, chosen, breadth):
    return jnp.take(rows.reshape(rows.shape[0], rows.shape[1] // breadth, breadth), chosen, axis=1)


def solve_rows(gram, rhs):
    components = gram.shape[0]
    matrix = gram / (jnp.trace(gram) / components) + 0.1 * jnp.eye(components, dtype=jnp.float32)
    lower = jnp.linalg.cholesky(matrix)
    return jax.scipy.linalg.cho_solve((lower, True), rhs)


def share_of(values, offset, length):
    return lax.dynamic_slice_in_dim(values, offset, length, 1)


def inner_gram(left_rows, right_rows):
    return jnp.dot(left_rows, right_rows.T, precision=HIGHEST)


def add_blocks(columns, chosen_blocks, alive, block_count):
    components = columns.shape[0]
    breadth = columns.shape[2]
    placed = jnp.zeros((components, block_count, breadth), jnp.float32)
    placed = placed.at[:, chosen_blocks, :].add(columns * alive[None, :, None])
    return placed.reshape(components, block_count * breadth)


def user_scale(value):
    return lax.psum(value, ("au", "ia"))


def user_gram(value):
    return lax.psum(value, ("au", "ia"))


def item_scale(value):
    return lax.psum(value, ("au", "ia"))


def item_gram(value):
    return lax.psum(value, ("au", "ia"))


def refresh(moments, prior_rows, gram_other, offset, length, entries, scale_sum, gram_sum):
    moment_share = share_of(moments, offset, length)
    squares = scale_sum(jnp.sum(moment_share * moment_share))
    norm_value = jnp.sqrt(squares / entries + EPSILON)
    factor = solve_rows(gram_other, moments / norm_value + prior_rows)
    factor_share = share_of(factor, offset, length)
    gram_new = gram_sum(inner_gram(factor_share, factor_share))
    return (factor, gram_new)


def sweep_tiles(tile_values, tile_index, live_count, worker, initial, stride, bound):

    def visit(turn, running):
        offset = turn * stride
        tile_block = lax.dynamic_slice_in_dim(tile_values, offset, stride, 0)
        chosen = lax.dynamic_slice_in_dim(tile_index, offset, stride, 1)
        alive = (offset + jnp.arange(stride, dtype=jnp.int32) < live_count).astype(jnp.float32)
        return running + worker(tile_block, chosen, alive)

    return lax.fori_loop(0, bound, visit, initial)


def shards(tile_values, tile_index, tile_count, user_prev, item_prev, day_prior):
    breadth = tile_values.shape[1]
    capacity = tile_values.shape[0]
    components = user_prev.shape[0]
    day_count = day_prior.shape[1]
    user_rows = user_prev.shape[1]
    item_rows = item_prev.shape[1]
    user_blocks = user_rows // breadth
    item_blocks = item_rows // breadth
    live_count = tile_count[0]
    stride = math.gcd(capacity, 32)
    bound = capacity // stride
    user_share = user_rows // lax.axis_size("ia")
    user_offset = lax.axis_index("ia") * user_share
    item_share = item_rows // lax.axis_size("au")
    item_offset = lax.axis_index("au") * item_share
    user_entries = components * user_rows * lax.axis_size("au")
    item_entries = components * item_rows * lax.axis_size("ia")
    users = user_prev
    items = item_prev
    users_part = share_of(users, user_offset, user_share)
    items_part = share_of(items, item_offset, item_share)
    gram_users = user_gram(inner_gram(users_part, users_part))
    gram_items = item_gram(inner_gram(items_part, items_part))
    day_factor = day_prior
    for turn in range(PASSES):
        users_half = users.astype(jnp.bfloat16)
        items_half = items.astype(jnp.bfloat16)

        def day_worker(tile_block, chosen, alive):
            user_part = pick_blocks(users_half, chosen[0], breadth)
            item_part = pick_blocks(items_half, chosen[1], breadth)
            partial_value = jnp.einsum(
                "rtu,tui->rti", user_part, tile_block, preferred_element_type=jnp.float32
            )
            weighed = (
                jnp.sum(partial_value * item_part.astype(jnp.float32), axis=2) * alive[None, :]
            )
            onehot = (chosen[2][:, None] == jnp.arange(day_count, dtype=jnp.int32)[None, :]).astype(
                jnp.float32
            )
            return jnp.dot(weighed, onehot, precision=HIGHEST)

        local_days = sweep_tiles(
            tile_values,
            tile_index,
            live_count,
            day_worker,
            jnp.zeros((components, day_count), jnp.float32),
            stride,
            bound,
        )
        moments = lax.psum(local_days, ("au", "ia"))
        norm_value = jnp.sqrt(jnp.mean(moments * moments) + EPSILON)
        day_factor = solve_rows(gram_users * gram_items, moments / norm_value + day_prior)
        gram_days = inner_gram(day_factor, day_factor)

        def user_worker(tile_block, chosen, alive):
            scaled = (
                pick_blocks(items, chosen[1], breadth) * day_factor[:, chosen[2]][:, :, None]
            ).astype(jnp.bfloat16)
            columns = jnp.einsum(
                "rti,tui->rtu", scaled, tile_block, preferred_element_type=jnp.float32
            )
            return add_blocks(columns, chosen[0], alive, user_blocks)

        local_users = sweep_tiles(
            tile_values,
            tile_index,
            live_count,
            user_worker,
            jnp.zeros((components, user_rows), jnp.float32),
            stride,
            bound,
        )
        moments = lax.psum(local_users, "ia")
        users, gram_users = refresh(
            moments,
            user_prev,
            gram_items * gram_days,
            user_offset,
            user_share,
            user_entries,
            user_scale,
            user_gram,
        )

        def item_worker(tile_block, chosen, alive):
            scaled = (
                pick_blocks(users, chosen[0], breadth) * day_factor[:, chosen[2]][:, :, None]
            ).astype(jnp.bfloat16)
            columns = jnp.einsum(
                "rtu,tui->rti", scaled, tile_block, preferred_element_type=jnp.float32
            )
            return add_blocks(columns, chosen[1], alive, item_blocks)

        local_items = sweep_tiles(
            tile_values,
            tile_index,
            live_count,
            item_worker,
            jnp.zeros((components, item_rows), jnp.float32),
            stride,
            bound,
        )
        moments = lax.psum(local_items, "au")
        items, gram_items = refresh(
            moments,
            item_prev,
            gram_users * gram_days,
            item_offset,
            item_share,
            item_entries,
            item_scale,
            item_gram,
        )
    return (users, items, day_factor)


def solution(mesh):
    return jax.shard_map(
        shards,
        mesh=mesh,
        in_specs=(
            P(("au", "ia"), None, None),
            P(None, ("au", "ia")),
            P(("au", "ia")),
            P(None, "au"),
            P(None, "ia"),
            P(),
        ),
        out_specs=(P(None, "au"), P(None, "ia"), P()),
        check_vma=False,
    )
```

profile of v0, /device:TPU:1, one launch (start us, length us, event | category | flops | bytes accessed | tf_op | source)
XLA Modules:
  0.0 1185.9 jit_solution(11405018129122446735)
XLA Ops:
  12.3 48.2 %while.84 = (s32[]{:T(128)}, f32[64,32]{0,1:T(8,128)S(1)}, bf16[256,128,128]{2,1,0:T(8,128)(2,1)}, bf16[64,4096]{1,0:T(8,128)(2,1)S(1)}, s32[3,256]{1,0:T(4,128)...) while((s32[]{:T(128)}, f32[64,32]{0,1:T(8,128)S(1)}, ...), condition=%wide.region_7.0_spmd.clone, body=%wide.region_5.9_spmd.clone.sunk | while | flops 69213672 | bytes 6335157 | solution.py:77
  60.5 69.5 %all-reduce.3 = (f32[64,64]{0,1:T(8,128)S(1)}, f32[64,64]{0,1:T(8,128)S(1)}, f32[64,32]{0,1:T(8,128)S(1)}) all-reduce(f32[64,64]{0,1:T(8,128)S(1)} %fusion.88, f32[64,64]{0,1:T(8,128)S(1)} %fusion.132, f32[64,32]{0,1:T(8,128)S(1)} %get-tuple-element.752), channel_id=1, replica_groups=mesh['au'=32,'ia'=4] {'au','ia'}, use_global_device_ids=true, to_apply=%region_1.0 | all-reduce | flops 10240 | bytes 81920 | tf_op jit(solution)/shard_map/psum | solution.py:47
  131.4 5.8 cholesky.104
  138.5 4.9 custom-call.22
  145.1 74.3 %while.85 = (s32[]{:T(128)}, f32[64,4096]{1,0:T(8,128)}, s32[3,256]{1,0:T(4,128)}, bf16[256,128,128]{2,1,0:T(8,128)(2,1)}, f32[64,4096]{1,0:T(8,128)S(1)}, /*ind...) while((s32[]{:T(128)}, f32[64,4096]{1,0:T(8,128)}, ...), condition=%wide.region_13.18_spmd.clone, body=%wide.region_11.17_spmd.clone.sunk | while | flops 68946408 | bytes 14715521 | solution.py:77
  221.1 5.8 cholesky.115
  228.3 32.3 %all-reduce.9.cloned.1.call-done = f32[64,4096]{1,0:T(8,128)} async-done(((f32[64,4096]{1,0:T(8,128)}), f32[64,4096]{1,0:T(8,128)}) %all-reduce.9.cloned.1.call-update) | async-done | bytes 1048592 | tf_op jit(solution)/shard_map/psum | solution.py:155
  267.1 66.7 %psum.109 = f32[]{:T(128)} all-reduce(f32[]{:T(128)} %multiply_reduce_fusion.1), channel_id=1, replica_groups=mesh['au'=32,'ia'=4] {'au','ia'}, use_global_device_ids=true, to_apply=%region_16.21 | all-reduce | flops 1 | bytes 8 | tf_op jit(solution)/shard_map/psum | solution.py:43
  338.9 71.9 %while.86 = (s32[]{:T(128)}, f32[64,4096]{1,0:T(8,128)}, s32[3,256]{1,0:T(4,128)}, bf16[256,128,128]{2,1,0:T(8,128)(2,1)}, f32[64,4096]{1,0:T(8,128)S(1)}, /*ind...) while((s32[]{:T(128)}, f32[64,4096]{1,0:T(8,128)}, ...), condition=%wide.region_21.27_spmd.clone, body=%wide.region_19.26_spmd.clone.sunk | while | flops 68946408 | bytes 14715521 | solution.py:77
  411.2 101.6 %all-reduce.11.cloned.1.call-done = f32[64,4096]{1,0:T(8,128)} async-done(((f32[64,4096]{1,0:T(8,128)}), f32[64,4096]{1,0:T(8,128)}) %all-reduce.11.cloned.1.call-update) | async-done | bytes 1048592 | tf_op jit(solution)/shard_map/psum | solution.py:185
  514.3 65.8 %all-reduce.2 = (f32[]{:T(128)}, f32[64,64]{0,1:T(8,128)S(1)}) all-reduce(f32[]{:T(128)} %multiply_reduce_fusion.3, f32[64,64]{0,1:T(8,128)S(1)} %fusion.86), channel_id=1, replica_groups=mesh['au'=32,'ia'=4] {'au','ia'}, use_global_device_ids=true, to_apply=%region_24.30 | all-reduce | flops 4097 | bytes 32776 | tf_op jit(solution)/shard_map/psum | solution.py:51
  581.4 5.8 cholesky.126
  597.8 49.5 %while.87 = (s32[]{:T(128)}, f32[64,32]{0,1:T(8,128)S(1)}, bf16[256,128,128]{2,1,0:T(8,128)(2,1)}, bf16[64,4096]{1,0:T(8,128)(2,1)}, s32[3,256]{1,0:T(4,128)}, /...) while((s32[]{:T(128)}, f32[64,32]{0,1:T(8,128)S(1)}, ...), condition=%wide.region_29.35_spmd.clone, body=%wide.region_27.34_spmd.clone.sunk | while | flops 69213672 | bytes 6335157 | solution.py:77
  647.4 63.4 %all-reduce.1 = (f32[64,64]{0,1:T(8,128)S(1)}, f32[64,32]{0,1:T(8,128)S(1)}) all-reduce(f32[64,64]{0,1:T(8,128)S(1)} %fusion.130, f32[64,32]{0,1:T(8,128)S(1)} %get-tuple-element.755), channel_id=1, replica_groups=mesh['au'=32,'ia'=4] {'au','ia'}, use_global_device_ids=true, to_apply=%region_25.31 | all-reduce | flops 6144 | bytes 49152 | tf_op jit(solution)/shard_map/psum | solution.py:55
  712.4 5.8 cholesky.137
  726.3 74.3 %while.88 = (s32[]{:T(128)}, f32[64,4096]{1,0:T(8,128)}, s32[3,256]{1,0:T(4,128)}, bf16[256,128,128]{2,1,0:T(8,128)(2,1)}, f32[64,4096]{1,0:T(8,128)S(1)}, /*ind...) while((s32[]{:T(128)}, f32[64,4096]{1,0:T(8,128)}, ...), condition=%wide.region_35.41_spmd.clone, body=%wide.region_33.40_spmd.clone.sunk | while | flops 68946408 | bytes 14715521 | solution.py:77
  802.4 5.8 cholesky.148
  809.7 32.4 %all-reduce.13.cloned.1.call-done = f32[64,4096]{1,0:T(8,128)} async-done(((f32[64,4096]{1,0:T(8,128)}), f32[64,4096]{1,0:T(8,128)}) %all-reduce.13.cloned.1.call-update) | async-done | bytes 1048592 | tf_op jit(solution)/shard_map/psum | solution.py:155
  848.6 66.5 %psum.116 = f32[]{:T(128)} all-reduce(f32[]{:T(128)} %multiply_reduce_fusion), channel_id=1, replica_groups=mesh['au'=32,'ia'=4] {'au','ia'}, use_global_device_ids=true, to_apply=%region_38.44 | all-reduce | flops 1 | bytes 8 | tf_op jit(solution)/shard_map/psum | solution.py:43
  919.4 71.4 %while.89 = (s32[]{:T(128)}, f32[64,4096]{1,0:T(8,128)}, s32[3,256]{1,0:T(4,128)}, bf16[256,128,128]{2,1,0:T(8,128)(2,1)}, f32[64,4096]{1,0:T(8,128)S(1)}, /*ind...) while((s32[]{:T(128)}, f32[64,4096]{1,0:T(8,128)}, ...), condition=%wide.region_43.49_spmd.clone, body=%wide.region_41.48_spmd.clone.sunk | while | flops 68946408 | bytes 14715521 | solution.py:77
  991.2 101.8 %all-reduce.15.cloned.1.call-done = f32[64,4096]{1,0:T(8,128)} async-done(((f32[64,4096]{1,0:T(8,128)}), f32[64,4096]{1,0:T(8,128)}) %all-reduce.15.cloned.1.call-update) | async-done | bytes 1048592 | tf_op jit(solution)/shard_map/psum | solution.py:185
  1094.3 65.8 %all-reduce = (f32[]{:T(128)}, f32[64,64]{0,1:T(8,128)S(1)}) all-reduce(f32[]{:T(128)} %multiply_reduce_fusion.2, f32[64,64]{0,1:T(8,128)S(1)} %fusion.84), channel_id=1, replica_groups=mesh['au'=32,'ia'=4] {'au','ia'}, use_global_device_ids=true, to_apply=%region_46.52 | all-reduce | flops 4097 | bytes 32776 | tf_op jit(solution)/shard_map/psum | solution.py:51
  1161.7 5.8 cholesky.159
  1169.0 4.9 custom-call.27
  (653 shorter events, 448.8 us)
Async XLA Ops:
  7.2 253.4 %all-reduce.9.cloned.1.call-start = ((), (), s32[]{:S(2)}) async-start(), calls=%async_computation | async-start | bytes 2097152 | tf_op jit(solution)/shard_map/psum | solution.py:155
  12.2 132.5 %copy-start.3 = (f32[64,32]{0,1:T(8,128)S(1)}, f32[64,32]{0,1:T(8,128)}, u32[]{:S(2)}) copy-start(f32[64,32]{0,1:T(8,128)} %param.32) | copy-start | bytes 24580
  12.2 132.8 %copy-start.2 = (f32[64,4096]{1,0:T(8,128)S(1)}, f32[64,4096]{1,0:T(8,128)}, u32[]{:S(2)}) copy-start(f32[64,4096]{1,0:T(8,128)} %param.31) | copy-start | bytes 3145732
  219.4 293.4 %all-reduce.11.cloned.1.call-start = ((), (), s32[]{:S(2)}) async-start(), calls=%async_computation.1 | async-start | bytes 2097152 | tf_op jit(solution)/shard_map/psum | solution.py:185
  410.8 431.3 %all-reduce.13.cloned.1.call-start = ((), (), s32[]{:S(2)}) async-start(), calls=%async_computation.2 | async-start | bytes 2097152 | tf_op jit(solution)/shard_map/psum | solution.py:155
  800.6 292.3 %all-reduce.15.cloned.1.call-start = ((), (), s32[]{:S(2)}) async-start(), calls=%async_computation.3 | async-start | bytes 2097152 | tf_op jit(solution)/shard_map/psum | solution.py:185
  990.8 188.4 %copy-start = (f32[64,32]{0,1:T(8,128)}, f32[64,32]{0,1:T(8,128)S(1)}, u32[]{:S(2)}) copy-start(f32[64,32]{0,1:T(8,128)S(1)} %get-tuple-element.1586) | copy-start | bytes 24580
  990.8 188.4 %copy-start.1 = (f32[64,4096]{1,0:T(8,128)}, f32[64,4096]{1,0:T(8,128)S(1)}, u32[]{:S(2)}) copy-start(f32[64,4096]{1,0:T(8,128)S(1)} %get-tuple-element.1593) | copy-start | bytes 3145732
Sparse Core Ops, SparseCore 0:
  219.5 40.9 all-reduce.8
  410.9 101.9 all-reduce.10
  800.8 41.2 all-reduce.12
  990.9 101.9 all-reduce.14
where the time goes:
time: 1200 us; the launch traced here: 1190 us
  blocking collectives  398 us (33%)
  waiting for transfers between devices  268 us (22%)
  other arithmetic  255 us (21%)
  local copies, waits for them, and re-layouts  122 us (10%)
  matrix products  116 us (10%)
  between operations  22.7 us (2%)
    psum x2, waiting for transfers between devices, shards(): moments = lax.psum(local_items, 'au')  203 us
    psum x2, blocking collectives, user_scale(): return lax.psum(value, ('au', 'ia'))  133 us
    psum x2, blocking collectives, item_scale(): return lax.psum(value, ('au', 'ia'))  132 us
    add x32, other arithmetic, visit(): return running + worker(tile_block, chosen, alive)  69.5 us
    psum x1, blocking collectives, user_gram(): return lax.psum(value, ('au', 'ia'))  69.5 us
    scatter-add x32, other arithmetic, add_blocks(): placed = placed.at[:, chosen_blocks, :].add(columns * alive[None, :, None])  68.1 us
    psum x2, waiting for transfers between devices, shards(): moments = lax.psum(local_users, 'ia')  64.6 us
    psum x1, blocking collectives, item_gram(): return lax.psum(value, ('au', 'ia'))  63.4 us
  transfers between devices with their start and end apart: 4, of which 4 were waited for; matrix products, arithmetic and copies ran while one was open for 1% of the time, Pallas kernels for 0%

commit v1 on v0

v1 whole, which is shorter than its diff:
```python
import functools

import jax
import jax.numpy as jnp
from jax import lax
from jax.experimental import pallas as pl
from jax.experimental.pallas import tpu as pltpu
from jax.sharding import PartitionSpec as P

PASSES = 2
R = 64
TILE = 128
DAYS = 32
BLOCKS = 32
CAP = 256
EPSILON = 1e-06
USER_ENTRIES = 64 * 131072
ITEM_ENTRIES = 64 * 16384
UNROLL = 8
MESH = pl.DeviceIdType.MESH
F32 = jnp.float32
BF16 = jnp.bfloat16

SUMS = 1 + 3 * PASSES
SCALES = 2 * PASSES

NN = (((1,), (0,)), ((), ()))
NT = (((1,), (1,)), ((), ()))


def mm(left, right, dims=NN):
    return lax.dot_general(left, right, dims, preferred_element_type=F32)


def halves(values):
    high = values.astype(BF16)
    return high, (values - high.astype(F32)).astype(BF16)


def mm3(left, right, dims=NN):
    lh, ll = halves(left)
    rh, rl = halves(right)
    return mm(lh, rh, dims) + (mm(lh, rl, dims) + mm(ll, rh, dims))


def rounds(generators):
    generators = list(generators)
    while generators:
        generators = [one for one in generators if next(one, "end") != "end"]


class Copies:
    def __init__(self, send, recv):
        self.send, self.recv, self.used = send, recv, 0

    def start(self, source, target, device):
        copy = pltpu.make_async_remote_copy(
            src_ref=source,
            dst_ref=target,
            send_sem=self.send.at[self.used],
            recv_sem=self.recv.at[self.used],
            device_id=device,
            device_id_type=MESH,
        )
        self.used += 1
        copy.start()
        return copy


COPIES = 10 * (SUMS + SCALES) + PASSES * (6 + 6 + 2 * (1 + 6 + 3))


def kernel(
    codes, last, tiles_hbm, user_prior, item_prior, day_prior,
    user_out, item_out, day_out,
    tiles, running, users, items, users_half, items_half, spread,
    mu, mi, t1u, t1i, t2,
    slots, scale_slots, urecv, irecv_core, irecv_one, irecv_two,
    tile_sem, send, recv,
):
    au = lax.axis_index("au")
    x = lax.axis_index("ia")
    core = lax.rem(au, 2)
    z = lax.rem(lax.div(au, 2), 4)
    y = lax.div(au, 8)

    def at(yy, zz, cc):
        return (yy * 4 + zz) * 2 + cc

    def along_x(step):
        return (au, lax.rem(x + step, 4))

    def along_y(step):
        return (at(lax.rem(y + step, 4), z, core), x)

    def along_z(step):
        return (at(y, lax.rem(z + step, 4), core), x)

    twin = (at(y, z, 1 - core), x)
    one = y * (1 - core) + z * core
    two = z * (1 - core) + y * core

    def along_one(step):
        new = lax.rem(one + step, 4)
        return (at(new * (1 - core) + y * core, z * (1 - core) + new * core, core), x)

    def along_two(step):
        new = lax.rem(two + step, 4)
        return (at(y * (1 - core) + new * core, new * (1 - core) + z * core, core), x)

    copies = Copies(send, recv)

    tile_copy = pltpu.make_async_copy(tiles_hbm, tiles, tile_sem)
    tile_copy.start()

    barrier = pltpu.get_barrier_semaphore()
    peers = [twin]
    for step in (1, 2, 3):
        peers += [along_x(step), along_y(step), along_z(step)]
    for peer in peers:
        pl.semaphore_signal(barrier, inc=1, device_id=peer, device_id_type=MESH)

    def total_over_all(where, value, result):
        where[core] = value
        copy = copies.start(where.at[core], where.at[core], twin)
        yield
        copy.wait()
        value = where[0] + where[1]
        base = 2
        for mine, along in ((x, along_x), (y, along_y), (z, along_z)):
            where[base + mine] = value
            flying = [
                copies.start(where.at[base + mine], where.at[base + mine], along(step))
                for step in (1, 2, 3)
            ]
            yield
            for copy in flying:
                copy.wait()
            value = (where[base] + where[base + 1]) + (where[base + 2] + where[base + 3])
            base += 4
        result.append(value)

    def reduce_ring(source, mine, along, width, got):
        half = width // 2

        def part(share, second):
            return pl.ds(lax.rem(share, 4) * width + second * half, half)

        far, right, left = mine + 2, mine + 1, mine + 3
        c1 = copies.start(source.at[part(far, 0)], got.at[0], along(3))
        c2 = copies.start(source.at[part(far, 1)], got.at[1], along(1))
        c3 = copies.start(source.at[part(left, 1)], got.at[2], along(3))
        c4 = copies.start(source.at[part(right, 0)], got.at[3], along(1))
        yield
        c1.wait()
        source[part(left, 0)] = source[part(left, 0)] + got[0]
        c5 = copies.start(source.at[part(left, 0)], got.at[4], along(3))
        c2.wait()
        source[part(right, 1)] = source[part(right, 1)] + got[1]
        c6 = copies.start(source.at[part(right, 1)], got.at[5], along(1))
        yield
        for copy in (c3, c4, c5, c6):
            copy.wait()
        source[part(mine, 0)] = source[part(mine, 0)] + (got[4] + got[3])
        source[part(mine, 1)] = source[part(mine, 1)] + (got[2] + got[5])

    def gather_ring(source, mine, along, width):
        half = width // 2

        def part(share, second):
            ref = source.at[pl.ds(lax.rem(share, 4) * width + second * half, half)]
            return ref

        left, right = mine + 3, mine + 1
        c1 = copies.start(part(mine, 0), part(mine, 0), along(1))
        c2 = copies.start(part(mine, 1), part(mine, 1), along(3))
        c3 = copies.start(part(mine, 1), part(mine, 1), along(1))
        c4 = copies.start(part(mine, 0), part(mine, 0), along(3))
        yield
        c1.wait()
        c5 = copies.start(part(left, 0), part(left, 0), along(1))
        c2.wait()
        c6 = copies.start(part(right, 1), part(right, 1), along(3))
        yield
        for copy in (c3, c4, c5, c6):
            copy.wait()

    def reduce_direct(source, base, mine, along, got):
        flying = [
            copies.start(source.at[base + lax.rem(mine + step, 4)], got.at[step - 1], along(step))
            for step in (1, 2, 3)
        ]
        yield
        for copy in flying:
            copy.wait()
        source[base + mine] = source[base + mine] + (got[0] + got[1] + got[2])

    def gather_direct(source, base, mine, along):
        here = source.at[base + mine]
        flying = [copies.start(here, here, along(step)) for step in (1, 2, 3)]
        yield
        for copy in flying:
            copy.wait()

    def inverse(gram):
        rows = lax.broadcasted_iota(jnp.int32, (R, 2 * R), 0)
        lanes = lax.broadcasted_iota(jnp.int32, (R, 2 * R), 1)
        diagonal = jnp.where(rows == lanes, 1.0, 0.0)
        trace = jnp.sum(jnp.sum(gram * diagonal[:, :R], axis=1, keepdims=True), axis=0, keepdims=True)
        matrix = gram / (trace / R) + 0.1 * diagonal[:, :R]
        matrix = jnp.concatenate([matrix, diagonal[:, :R]], axis=1)

        def eight(_, matrix):
            for k in range(8):
                pivot = matrix[k : k + 1, k : k + 1]
                row = matrix[k : k + 1, :] / pivot
                column = matrix[:, k : k + 1] - jnp.where(rows[:, :1] == k, 1.0, 0.0)
                matrix = matrix - column * row
            matrix = jnp.concatenate([matrix[8:], matrix[:8]], axis=0)
            return pltpu.roll(matrix, 2 * R - 8, 1)

        return lax.fori_loop(0, R // 8, eight, matrix)[:, :R]

    def sweep(order, product, begin=0, end=CAP, acc=None):
        def visit(turn, acc):
            for k in range(UNROLL):
                place = turn * UNROLL + k
                code = codes[order, place]
                slot = code & 255
                ub = (code >> 8) & 31
                ib = (code >> 13) & 31
                day = (code >> 18) & 31
                keep = (1 - (code >> 23)).astype(F32)
                acc = acc * keep + product(tiles[slot], ub, ib, day)
                running[place] = acc
            return acc

        if acc is None:
            acc = jnp.zeros((R, TILE), F32)
        return lax.fori_loop(begin // UNROLL, end // UNROLL, visit, acc)

    def assemble(order, target):
        def visit(block, carry):
            target[block] = running[last[order, block]]
            return carry

        lax.fori_loop(0, BLOCKS, visit, 0)

    def gram_part(values):
        high, low = halves(values)
        cross = mm(high, low, NT)
        return mm(high, high, NT) + (cross + mm(low, high, NT))

    def user_gram_part():
        def visit(step, total):
            return total + gram_part(users[x * 8 + step])

        return lax.fori_loop(0, 8, visit, jnp.zeros((R, R), F32))

    def item_gram_part():
        return gram_part(items[core * 16 + one * 4 + two])

    def pair(left, right):
        return jnp.concatenate([left, right], axis=1)

    def squares(source, begin, count):
        total = jnp.zeros((8, TILE), F32)
        for step in range(count):
            value = source[begin + step]
            value = value * value
            total = total + jnp.sum(value.reshape(8, 8, TILE), axis=0)
        return total

    def scale_of(total, entries):
        total = jnp.sum(jnp.sum(total, axis=1, keepdims=True), axis=0, keepdims=True)
        return jnp.sqrt(total / entries + EPSILON)

    def prior_part(inv, prior):
        def visit(block, carry):
            t2[block] = mm3(inv, prior[:, pl.ds(pl.multiple_of(block * TILE, TILE), TILE)])
            return carry

        lax.fori_loop(0, BLOCKS, visit, 0)

    def apply(inv, source, begin, count, target):
        for step in range(count):
            target[begin + step] = mm3(inv, source[begin + step])

    def finish(target, target_half, t1, norm, out):
        def visit(block, carry):
            value = t1[block] / norm + t2[block]
            target[block] = value
            target_half[block] = value.astype(BF16)
            if out is not None:
                out[:, pl.ds(pl.multiple_of(block * TILE, TILE), TILE)] = value
            return carry

        lax.fori_loop(0, BLOCKS, visit, 0)

    def lay(block, carry):
        columns = pl.ds(pl.multiple_of(block * TILE, TILE), TILE)
        value = user_prior[:, columns]
        users[block] = value
        users_half[block] = value.astype(BF16)
        value = item_prior[:, columns]
        items[block] = value
        items_half[block] = value.astype(BF16)
        return carry

    lax.fori_loop(0, BLOCKS, lay, 0)
    running[CAP] = jnp.zeros((R, TILE), F32)
    first = pair(user_gram_part(), item_gram_part())

    pl.semaphore_wait(barrier, len(peers))
    found = []
    rounds([total_over_all(slots.at[0], first, found)])
    gram_users, gram_items = found[0][:, :R], found[0][:, R:]
    tile_copy.wait()

    for turn in range(PASSES):
        final = turn == PASSES - 1

        def day_product(tile, ub, ib, day):
            return mm(users_half[ub], tile) * items_half[ib].astype(F32)

        sweep(2, day_product)
        lanes = lax.broadcasted_iota(jnp.int32, (R, TILE), 1)

        def day_sum(day, total):
            value = jnp.sum(running[last[2, day]], axis=1, keepdims=True)
            return jnp.where(lanes == day, value, total)

        moments = lax.fori_loop(0, DAYS, day_sum, jnp.zeros((R, TILE), F32))
        found = []
        job = total_over_all(slots.at[1 + 3 * turn], moments, found)
        next(job)
        inv = inverse(gram_users * gram_items)
        rounds([job])
        moments = found[0][:, :DAYS]
        square = moments * moments
        square = jnp.sum(jnp.sum(square, axis=1, keepdims=True), axis=0, keepdims=True)
        norm = jnp.sqrt(square / (R * DAYS) + EPSILON)
        days = mm3(inv, moments / norm + day_prior[...])
        gram_days = gram_part(days)
        if final:
            day_out[...] = days
        for day in range(DAYS):
            spread[day] = jnp.broadcast_to(days[:, day : day + 1], (R, TILE))

        def user_product(tile, ub, ib, day):
            return mm((items[ib] * spread[day]).astype(BF16), tile, NT)

        sweep(0, user_product)
        assemble(0, mu)
        job = reduce_ring(mu, x, along_x, 8, urecv.at[turn])
        next(job)
        inv = inverse(gram_items * gram_days)
        next(job)
        prior_part(inv, user_prior)
        rounds([job])
        found = []
        apply(inv, mu, x * 8, 8, t1u.at[turn])
        rounds([
            gather_ring(t1u.at[turn], x, along_x, 8),
            total_over_all(scale_slots.at[2 * turn], squares(mu, x * 8, 8), found),
        ])
        finish(users, users_half, t1u.at[turn], scale_of(found[0], USER_ENTRIES), user_out if final else None)

        found = []
        job = total_over_all(slots.at[2 + 3 * turn], pair(user_gram_part(), jnp.zeros((R, R), F32)), found)
        next(job)

        def item_product(tile, ub, ib, day):
            return mm((users[ub] * spread[day]).astype(BF16), tile)

        sweep(1, item_product)
        assemble(1, mi)
        rounds([job])
        gram_users = found[0][:, :R]
        other = 16 - core * 16
        copy = copies.start(mi.at[pl.ds(other, 16)], irecv_core.at[turn], twin)
        inv = inverse(gram_users * gram_days)
        copy.wait()
        own = pl.ds(core * 16, 16)
        mi[own] = mi[own] + irecv_core[turn]
        job = reduce_ring(mi.at[own], one, along_one, 4, irecv_one.at[turn])
        next(job)
        prior_part(inv, item_prior)
        rounds([job])
        base = core * 16 + one * 4
        rounds([reduce_direct(mi, base, two, along_two, irecv_two.at[turn])])
        found = []
        apply(inv, mi, base + two, 1, t1i.at[turn])
        scale_job = total_over_all(scale_slots.at[2 * turn + 1], squares(mi, base + two, 1), found)
        next(scale_job)
        rounds([gather_direct(t1i.at[turn], base, two, along_two)])
        rounds([gather_ring(t1i.at[turn, own], one, along_one, 4), scale_job])
        copy = copies.start(t1i.at[turn, own], t1i.at[turn, own], twin)
        copy.wait()
        finish(items, items_half, t1i.at[turn], scale_of(found[0], ITEM_ENTRIES), item_out if final else None)
        if not final:
            found = []
            job = total_over_all(slots.at[3 + 3 * turn], pair(item_gram_part(), jnp.zeros((R, R), F32)), found)
            rounds([job])
            gram_items = found[0][:, :R]


def sorted_codes(tile_index, tile_count):
    slot = jnp.arange(CAP, dtype=jnp.int32)
    live = slot < tile_count[0]
    keys = jnp.where(live[None, :], tile_index, BLOCKS)
    unique = keys * CAP + slot[None, :]
    before = unique[:, None, :] < unique[:, :, None]
    same = keys[:, None, :] == keys[:, :, None]
    rank = jnp.sum(before.astype(jnp.int32), axis=2)
    follows = jnp.sum((before & same).astype(jnp.int32), axis=2) > 0
    code = slot + tile_index[0] * 256 + tile_index[1] * 8192 + tile_index[2] * 262144
    code = code[None, :] + jnp.where(follows, 0, 1 << 23)
    codes = jnp.sum(jnp.where(rank[:, None, :] == slot[None, :, None], code[:, None, :], 0), axis=2)
    block = jnp.arange(BLOCKS, dtype=jnp.int32)[None, :, None]
    upto = jnp.sum((keys[:, None, :] <= block).astype(jnp.int32), axis=2)
    count = jnp.sum((keys[:, None, :] == block).astype(jnp.int32), axis=2)
    return codes, jnp.where(count > 0, upto - 1, CAP)


def shards(tile_values, tile_index, tile_count, user_prev, item_prev, day_prior):
    codes, last = sorted_codes(tile_index, tile_count)
    vmem = pl.BlockSpec(memory_space=pltpu.VMEM)
    smem = pl.BlockSpec(memory_space=pltpu.SMEM)
    block = (BLOCKS, R, TILE)
    return pl.pallas_call(
        kernel,
        out_shape=(
            jax.ShapeDtypeStruct(user_prev.shape, F32),
            jax.ShapeDtypeStruct(item_prev.shape, F32),
            jax.ShapeDtypeStruct(day_prior.shape, F32),
        ),
        in_specs=[smem, smem, pl.BlockSpec(memory_space=pl.ANY), vmem, vmem, vmem],
        out_specs=(vmem, vmem, vmem),
        scratch_shapes=[
            pltpu.VMEM((CAP, TILE, TILE), BF16),
            pltpu.VMEM((CAP + 1, R, TILE), F32),
            pltpu.VMEM(block, F32),
            pltpu.VMEM(block, F32),
            pltpu.VMEM(block, BF16),
            pltpu.VMEM(block, BF16),
            pltpu.VMEM(block, F32),
            pltpu.VMEM(block, F32),
            pltpu.VMEM(block, F32),
            pltpu.VMEM((PASSES, *block), F32),
            pltpu.VMEM((PASSES, *block), F32),
            pltpu.VMEM(block, F32),
            pltpu.VMEM((SUMS, 14, R, TILE), F32),
            pltpu.VMEM((SCALES, 14, 8, TILE), F32),
            pltpu.VMEM((PASSES, 6, 4, R, TILE), F32),
            pltpu.VMEM((PASSES, 16, R, TILE), F32),
            pltpu.VMEM((PASSES, 6, 2, R, TILE), F32),
            pltpu.VMEM((PASSES, 3, R, TILE), F32),
            pltpu.SemaphoreType.DMA,
            pltpu.SemaphoreType.DMA((COPIES,)),
            pltpu.SemaphoreType.DMA((COPIES,)),
        ],
        compiler_params=pltpu.CompilerParams(
            collective_id=0, has_side_effects=True, vmem_limit_bytes=60 * 1024 * 1024
        ),
    )(codes, last, tile_values, user_prev, item_prev, day_prior)


def solution(mesh):
    return jax.shard_map(
        shards,
        mesh=mesh,
        in_specs=(
            P(("au", "ia"), None, None),
            P(None, ("au", "ia")),
            P(("au", "ia")),
            P(None, "au"),
            P(None, "ia"),
            P(),
        ),
        out_specs=(P(None, "au"), P(None, "ia"), P()),
        check_vma=False,
    )
```

time: 1200 us -> 298 us (0.25); the launches traced: 1190 us -> 297 us
  blocking collectives: 398 us -> 0 us
  Pallas kernels: 0 us -> 285 us
  waiting for transfers between devices: 268 us -> 0 us
  other arithmetic: 255 us -> 3.6 us
  matrix products: 116 us -> 0 us
  local copies, waits for them, and re-layouts: 122 us -> 7.39 us
  between operations: 22.7 us -> 1.3 us
    psum x6 -> x0, blocking collectives: 398 us -> none  [the longest x2 133 us: user_scale(): return lax.psum(value, ('au', 'ia'))]
    pallas_call x0 -> x1, Pallas kernels: none -> 285 us  [shards(): pl.pallas_call(kernel, out_shape=(jax.ShapeDtypeStruct(user_prev.shape, F...]
    psum x4 -> x0, waiting for transfers between devices: 268 us -> none  [the longest x2 203 us: shards(): moments = lax.psum(local_items, 'au')]
    dot_general x71 -> x0, matrix products: 99.7 us -> none  [the longest x16 33.3 us: user_worker(): jnp.einsum('rti,tui->rtu', scaled, tile_block, preferred_element_type=jnp...]
    another operation x30 -> x0, other arithmetic: 72.7 us -> none  [the longest x18 39.3 us: solve_rows(): lower = jnp.linalg.cholesky(matrix)]
    scatter-add x32 -> x0, other arithmetic: 68.1 us -> none  [add_blocks(): placed = placed.at[:, chosen_blocks, :].add(columns * alive[None, :, None])]
    add x38 -> x3, other arithmetic: 69.6 us -> 1.5 us  [the longest x1 0.81 us: sorted_codes(): slot + tile_index[0] * 256 + tile_index[1] * 8192 + tile_index[2] * 262144]
    gather x96 -> x0, local copies, waits for them, and re-layouts: 65.1 us -> none  [the longest x64 46.7 us: pick_blocks(): jnp.take(rows.reshape(rows.shape[0], rows.shape[1] // breadth, breadth),...]
  transfers between devices with their start and end apart: 4 -> 0, of which waited for: 4 -> 0; matrix products, arithmetic and copies ran while one was open for 1% -> 0% of each run, Pallas kernels for 0% -> 0%
where the time goes in v1:
time: 298 us; the launch traced here: 297 us
  Pallas kernels  285 us (96%)
  local copies, waits for them, and re-layouts  7.39 us (2%)
  other arithmetic  3.6 us (1%)
    pallas_call x1, Pallas kernels, shards(): pl.pallas_call(kernel, out_shape=(jax.ShapeDtypeStruct(user_prev.shape, F...  285 us

profile of v1, /device:TPU:1, one launch (start us, length us, event | category | flops | bytes accessed | tf_op | source)
XLA Modules:
  0.0 297.3 jit_solution(15388654054420780315)
XLA Ops:
  1.3 0.8 multiply_add_fusion
  2.1 0.7 iota_add_fusion
  2.8 0.5 fusion
  3.3 0.2 convert_reduce_fusion.2
  3.5 0.6 add_select_fusion.last
  4.1 0.8 select_reduce_fusion.codes
  4.9 1.4 copy.11.day_prior
  6.3 285.0 %shard_map.85 = (f32[64,4096]{1,0:T(8,128)}, f32[64,4096]{1,0:T(8,128)}, f32[64,32]{1,0:T(8,128)}) custom-call(s32[3,256]{1,0:T(4,128)} %select_reduce_fusion.codes, s32[3,32]{1,0:T(4,128)} %add_select_fusion.last, bf16[256,128,128]{2,1,0:T(8,128)(2,1)} %tiles_hbm.1, f32[64,4096]{1,0:T(8,128)} %user_prior.1, f32[64,4096]{1,0:T(8,128)} %item_prior.1, ...), custom_call_target="tpu_custom_call" | custom-call | tf_op jit(solution)/shard_map/pallas_call | solution.py:431
  291.3 1.4 copy.12
  292.8 2.3 copy.16
  295.1 2.3 copy.17
  (2 shorter events, 0.0 us)

commit v2 on v1

v2 whole, which is shorter than its diff:
```python
import functools

import jax
import jax.numpy as jnp
from jax import lax
from jax.experimental import pallas as pl
from jax.experimental.pallas import tpu as pltpu
from jax.sharding import PartitionSpec as P

PASSES = 2
R = 64
TILE = 128
DAYS = 32
BLOCKS = 32
CAP = 256
EPSILON = 1e-06
USER_ENTRIES = 64 * 131072
ITEM_ENTRIES = 64 * 16384
UNROLL = 32
MESH = pl.DeviceIdType.MESH
F32 = jnp.float32
BF16 = jnp.bfloat16

NN = (((1,), (0,)), ((), ()))
NT = (((1,), (1,)), ((), ()))


def mm(left, right, dims=NN):
    return lax.dot_general(left, right, dims, preferred_element_type=F32)


def halves(values):
    high = values.astype(BF16)
    return high, (values - high.astype(F32)).astype(BF16)


def left_three(values):
    high, low = halves(values)
    return jnp.concatenate([high, high, low], axis=1)


def right_three(values):
    high, low = halves(values)
    return jnp.concatenate([high, low, high], axis=0)


def drain(job):
    for _ in job:
        pass


class Copies:
    def __init__(self, send, recv):
        self.send, self.recv, self.used = send, recv, 0

    def start(self, source, target, device):
        copy = pltpu.make_async_remote_copy(
            src_ref=source,
            dst_ref=target,
            send_sem=self.send.at[self.used],
            recv_sem=self.recv.at[self.used],
            device_id=device,
            device_id_type=MESH,
        )
        self.used += 1
        copy.start()
        return copy


COPIES = 7 + 7 * (PASSES - 1) + 7 + 3 * PASSES + PASSES * (19 + 19 + 19 + 6 + 6 + 1 + 15 + 15 + 1)


def kernel(
    codes, last, tiles_hbm, user_prior, item_prior, day_prior,
    user_out, item_out, day_out,
    tiles, tiles_t, running, users, items, users_half, items_half, spread,
    mu, mi, t1u, t1i, t2,
    gu_slots, gv_slots, md_slots, scale_slots, urecv, irecv_core, irecv,
    tile_sem, send, recv,
):
    au = lax.axis_index("au")
    x = lax.axis_index("ia")
    core = lax.rem(au, 2)
    z = lax.rem(lax.div(au, 2), 4)
    y = lax.div(au, 8)
    plane = y * 4 + z

    def at(yy, zz, cc):
        return (yy * 4 + zz) * 2 + cc

    twin = (at(y, z, 1 - core), x)

    def along_x(step):
        return (au, lax.rem(x + step, 4))

    def along_y(step):
        return (at(lax.rem(y + step, 4), z, core), x)

    def along_z(step):
        return (at(y, lax.rem(z + step, 4), core), x)

    def along_yz(step):
        yy, zz = lax.rem(y + step // 4, 4), lax.rem(z + step % 4, 4)
        return (at(yy, zz, core), x)

    def plane_of(step):
        return lax.rem(y + step // 4, 4) * 4 + lax.rem(z + step % 4, 4)

    kinds = {
        "core": (2, core, lambda step: twin),
        "x": (4, x, along_x),
        "y": (4, y, along_y),
        "z": (4, z, along_z),
        "yz": (16, plane, along_yz),
    }

    copies = Copies(send, recv)

    tile_copy = pltpu.make_async_copy(tiles_hbm, tiles, tile_sem)
    tile_copy.start()

    barrier = pltpu.get_barrier_semaphore()
    peers = [twin] + [along_x(step) for step in (1, 2, 3)] + [along_yz(step) for step in range(1, 16)]
    for peer in peers:
        pl.semaphore_signal(barrier, inc=1, device_id=peer, device_id_type=MESH)

    def total_over(stages, where, value, result):
        base = 0
        for stage in stages:
            size, mine, along = kinds[stage]
            here = where.at[base + mine]
            where[base + mine] = value
            flying = [copies.start(here, here, along(step)) for step in range(1, size)]
            yield
            for copy in flying:
                copy.wait()
            terms = [where[base + place] for place in range(size)]
            while len(terms) > 1:
                terms = [terms[k] + terms[k + 1] for k in range(0, len(terms), 2)]
            value = terms[0]
            base += size
        result.append(value)

    def reduce_ring(source, mine, along, width, got):
        half = width // 2

        def part(share, second):
            return pl.ds(lax.rem(share, 4) * width + second * half, half)

        far, right, left = mine + 2, mine + 1, mine + 3
        c1 = copies.start(source.at[part(far, 0)], got.at[0], along(3))
        c2 = copies.start(source.at[part(far, 1)], got.at[1], along(1))
        c3 = copies.start(source.at[part(left, 1)], got.at[2], along(3))
        c4 = copies.start(source.at[part(right, 0)], got.at[3], along(1))
        yield
        c1.wait()
        source[part(left, 0)] = source[part(left, 0)] + got[0]
        c5 = copies.start(source.at[part(left, 0)], got.at[4], along(3))
        c2.wait()
        source[part(right, 1)] = source[part(right, 1)] + got[1]
        c6 = copies.start(source.at[part(right, 1)], got.at[5], along(1))
        yield
        for copy in (c3, c4, c5, c6):
            copy.wait()
        source[part(mine, 0)] = source[part(mine, 0)] + (got[4] + got[3])
        source[part(mine, 1)] = source[part(mine, 1)] + (got[2] + got[5])

    def gather_ring(source, mine, along, width):
        half = width // 2

        def part(share, second):
            return source.at[pl.ds(lax.rem(share, 4) * width + second * half, half)]

        left, right = mine + 3, mine + 1
        c1 = copies.start(part(mine, 0), part(mine, 0), along(1))
        c2 = copies.start(part(mine, 1), part(mine, 1), along(3))
        c3 = copies.start(part(mine, 1), part(mine, 1), along(1))
        c4 = copies.start(part(mine, 0), part(mine, 0), along(3))
        yield
        c1.wait()
        c5 = copies.start(part(left, 0), part(left, 0), along(1))
        c2.wait()
        c6 = copies.start(part(right, 1), part(right, 1), along(3))
        yield
        for copy in (c3, c4, c5, c6):
            copy.wait()

    def reduce_plane(source, base, got):
        flying = [
            copies.start(source.at[base + plane_of(step)], got.at[step - 1], along_yz(step))
            for step in range(1, 16)
        ]
        yield
        for copy in flying:
            copy.wait()
        total = source[base + plane]
        for step in range(15):
            total = total + got[step]
        source[base + plane] = total

    def gather_plane(source, base):
        here = source.at[base + plane]
        flying = [copies.start(here, here, along_yz(step)) for step in range(1, 16)]
        yield
        for copy in flying:
            copy.wait()

    def inverse(gram):
        rows = lax.broadcasted_iota(jnp.int32, (R, 2 * R), 0)
        lanes = lax.broadcasted_iota(jnp.int32, (R, 2 * R), 1)
        diagonal = jnp.where(rows == lanes, 1.0, 0.0)
        trace = jnp.sum(jnp.sum(gram * diagonal[:, :R], axis=1, keepdims=True), axis=0, keepdims=True)
        matrix = gram / (trace / R) + 0.1 * diagonal[:, :R]
        matrix = jnp.concatenate([matrix, diagonal[:, :R]], axis=1)

        def eight(_, matrix):
            for k in range(8):
                pivot = matrix[k : k + 1, k : k + 1]
                row = matrix[k : k + 1, :] / pivot
                column = matrix[:, k : k + 1] - jnp.where(rows[:, :1] == k, 1.0, 0.0)
                matrix = matrix - column * row
            matrix = jnp.concatenate([matrix[8:], matrix[:8]], axis=0)
            return pltpu.roll(matrix, 2 * R - 8, 1)

        return left_three(lax.fori_loop(0, R // 8, eight, matrix)[:, :R])

    def sweep(order, source, product, begin=0, end=CAP, acc=None):
        def visit(turn, acc):
            for k in range(UNROLL):
                place = turn * UNROLL + k
                code = codes[order, place]
                slot = code & 255
                ub = (code >> 8) & 31
                ib = (code >> 13) & 31
                day = (code >> 18) & 31
                keep = (1 - (code >> 23)).astype(F32)
                acc = acc * keep + product(source[slot], ub, ib, day)
                running[place] = acc
            return acc

        if acc is None:
            acc = jnp.zeros((R, TILE), F32)
        return lax.fori_loop(begin // UNROLL, end // UNROLL, visit, acc)

    def each_block(visit, by=4):
        def some(step, carry):
            for k in range(by):
                visit(step * by + k)
            return carry

        lax.fori_loop(0, BLOCKS // by, some, 0)

    def columns(block):
        return pl.ds(pl.multiple_of(block * TILE, TILE), TILE)

    def assemble(order, target):
        def visit(block):
            target[block] = running[last[order, block]]

        each_block(visit, 8)

    def gram_of(source):
        def four(step, carry):
            total, cross = carry
            for k in range(2):
                block = step * 4 + k * 2
                high, low = halves(jnp.concatenate([source[block], source[block + 1]], axis=1))
                total = total + mm(high, high, NT)
                cross = cross + mm(high, low, NT)
            return total, cross

        zero = jnp.zeros((R, R), F32)
        total, cross = lax.fori_loop(0, BLOCKS // 4, four, (zero, zero))
        return total + (cross + cross.T)

    def fold(gram):
        return jnp.concatenate([gram[: R // 2], gram[R // 2 :]], axis=1)

    def unfold(value):
        return jnp.concatenate([value[:, :R], value[:, R:]], axis=0)

    def squares(source, begin, count):
        total = jnp.zeros((8, TILE), F32)
        for step in range(count):
            value = source[begin + step]
            value = value * value
            total = total + jnp.sum(value.reshape(8, 8, TILE), axis=0)
        return total

    def scale_of(total, entries):
        total = jnp.sum(jnp.sum(total, axis=1, keepdims=True), axis=0, keepdims=True)
        return jnp.sqrt(total / entries + EPSILON)

    def prior_part(inv, prior):
        def visit(step, carry):
            wide = prior[:, pl.ds(pl.multiple_of(step * 4 * TILE, 4 * TILE), 4 * TILE)]
            wide = mm(inv, right_three(wide))
            for k in range(4):
                t2[step * 4 + k] = wide[:, k * TILE : (k + 1) * TILE]
            return carry

        lax.fori_loop(0, BLOCKS // 4, visit, 0)

    def apply(inv, source, begin, count, target):
        for step in range(count):
            target[begin + step] = mm(inv, right_three(source[begin + step]))

    def finish(target, target_half, t1, norm, out):
        share = 1.0 / norm

        def visit(block):
            value = t1[block] * share + t2[block]
            target[block] = value
            target_half[block] = value.astype(BF16)
            if out is not None:
                out[:, columns(block)] = value

        each_block(visit)

    def lay(block):
        value = user_prior[:, columns(block)]
        users[block] = value
        users_half[block] = value.astype(BF16)
        value = item_prior[:, columns(block)]
        items[block] = value
        items_half[block] = value.astype(BF16)

    each_block(lay)
    running[CAP] = jnp.zeros((R, TILE), F32)
    gu_part, gv_part = fold(gram_of(users)), fold(gram_of(items))
    day_rows = day_prior[...].T
    lanes = lax.broadcasted_iota(jnp.int32, (R, TILE), 1)

    def transpose_tiles(begin, end):
        def visit(step, carry):
            for k in range(16):
                tiles_t[step * 16 + k] = tiles[step * 16 + k].T
            return carry

        lax.fori_loop(begin // 16, end // 16, visit, 0)

    pl.semaphore_wait(barrier, len(peers))
    gu_found = []
    gu_job = total_over(("core", "y", "z"), gu_slots.at[0], gu_part, gu_found)
    next(gu_job)

    for turn in range(PASSES):
        final = turn == PASSES - 1

        gv_found = []
        gv_job = total_over(("x",), gv_slots.at[turn], gv_part, gv_found)
        next(gv_job)
        if turn == 0:
            tile_copy.wait()

        def day_product(tile, ub, ib, day):
            return mm(users_half[ub], tile) * items_half[ib].astype(F32)

        acc = sweep(2, tiles, day_product, 0, CAP // 2)
        if turn == 0:
            next(gu_job)
        sweep(2, tiles, day_product, CAP // 2, CAP, acc)

        def day_sums(step, total):
            for k in range(8):
                day = step * 8 + k
                value = jnp.sum(running[last[2, day]], axis=1, keepdims=True)
                total = jnp.where(lanes == day, value, total)
            return total

        moments = lax.fori_loop(0, DAYS // 8, day_sums, jnp.zeros((R, TILE), F32))
        moments = (moments[:16] + pltpu.roll(moments[16:32], 32, 1)) + (
            pltpu.roll(moments[32:48], 64, 1) + pltpu.roll(moments[48:], 96, 1)
        )
        md_found = []
        md_job = total_over(("core", "x", "yz"), md_slots.at[turn], moments, md_found)
        next(md_job)
        next(md_job)
        if turn == 0:
            next(gu_job)
            transpose_tiles(0, CAP // 2)
            next(md_job)
            transpose_tiles(CAP // 2, CAP)
            drain(gu_job)
            gram_users = unfold(gu_found[0])
            drain(gv_job)
            gram_items = unfold(gv_found[0])
            inv = inverse(gram_users * gram_items)
        else:
            drain(gv_job)
            gram_items = unfold(gv_found[0])
            inv = inverse(gram_users * gram_items)
            next(md_job)
        drain(md_job)
        moments = md_found[0]
        square = moments * moments
        square = jnp.sum(jnp.sum(square, axis=1, keepdims=True), axis=0, keepdims=True)
        norm = jnp.sqrt(square / (R * DAYS) + EPSILON)
        moments = moments / norm
        moments = jnp.concatenate(
            [moments[:, :DAYS]] + [pltpu.roll(moments, TILE - k * 32, 1)[:, :DAYS] for k in (1, 2, 3)], axis=0
        )
        days = mm(inv, right_three(moments + day_rows))
        for day in range(DAYS):
            spread[day] = jnp.broadcast_to(days[:, day : day + 1], (R, TILE))
        high, low = halves(days)
        cross = mm(high, low, NT)
        gram_days = mm(high, high, NT) + (cross + mm(low, high, NT))
        if final:
            day_out[...] = days.T

        def user_product(tile, ub, ib, day):
            return mm((items[ib] * spread[day]).astype(BF16), tile)

        sweep(0, tiles_t, user_product)
        assemble(0, mu)
        job = reduce_ring(mu, x, along_x, 8, urecv.at[turn])
        next(job)
        inv = inverse(gram_items * gram_days)
        drain(job)
        apply(inv, mu, x * 8, 8, t1u.at[turn])
        job = gather_ring(t1u.at[turn], x, along_x, 8)
        next(job)
        scale_found = []
        scale_job = total_over(
            ("core", "yz", "x"), scale_slots.at[turn, 0], squares(mu, x * 8, 8), scale_found
        )
        next(scale_job)
        next(scale_job)
        prior_part(inv, user_prior)
        next(job)
        next(scale_job)
        drain(scale_job)
        drain(job)
        finish(users, users_half, t1u.at[turn], scale_of(scale_found[0], USER_ENTRIES), user_out if final else None)

        gu_found = []
        gu_job = total_over(("core", "y", "z"), gu_slots.at[1 + turn], fold(gram_of(users)), gu_found)
        next(gu_job)

        def item_product(tile, ub, ib, day):
            return mm((users[ub] * spread[day]).astype(BF16), tile)

        acc = sweep(1, tiles, item_product, 0, CAP // 2)
        next(gu_job)
        sweep(1, tiles, item_product, CAP // 2, CAP, acc)
        assemble(1, mi)
        own, other = pl.ds(core * 16, 16), pl.ds(16 - core * 16, 16)
        copy = copies.start(mi.at[other], irecv_core.at[turn], twin)
        copy.wait()
        mi[own] = mi[own] + irecv_core[turn]
        job = reduce_plane(mi, core * 16, irecv.at[turn])
        next(job)
        drain(gu_job)
        gram_users = unfold(gu_found[0])
        inv = inverse(gram_users * gram_days)
        drain(job)
        apply(inv, mi, core * 16 + plane, 1, t1i.at[turn])
        job = gather_plane(t1i.at[turn], core * 16)
        next(job)
        scale_found = []
        scale_job = total_over(
            ("x", "yz", "core"), scale_slots.at[turn, 1], squares(mi, core * 16 + plane, 1), scale_found
        )
        next(scale_job)
        prior_part(inv, item_prior)
        next(scale_job)
        drain(job)
        copy = copies.start(t1i.at[turn, own], t1i.at[turn, own], twin)
        drain(scale_job)
        copy.wait()
        finish(items, items_half, t1i.at[turn], scale_of(scale_found[0], ITEM_ENTRIES), item_out if final else None)
        if not final:
            gv_part = fold(gram_of(items))


def sorted_codes(tile_index, tile_count):
    slot = jnp.arange(CAP, dtype=jnp.int32)
    live = slot < tile_count[0]
    keys = jnp.where(live[None, :], tile_index, BLOCKS)
    unique = keys * CAP + slot[None, :]
    before = unique[:, None, :] < unique[:, :, None]
    same = keys[:, None, :] == keys[:, :, None]
    rank = jnp.sum(before.astype(jnp.int32), axis=2)
    follows = jnp.sum((before & same).astype(jnp.int32), axis=2) > 0
    code = slot + tile_index[0] * 256 + tile_index[1] * 8192 + tile_index[2] * 262144
    code = code[None, :] + jnp.where(follows, 0, 1 << 23)
    codes = jnp.sum(jnp.where(rank[:, None, :] == slot[None, :, None], code[:, None, :], 0), axis=2)
    block = jnp.arange(BLOCKS, dtype=jnp.int32)[None, :, None]
    upto = jnp.sum((keys[:, None, :] <= block).astype(jnp.int32), axis=2)
    count = jnp.sum((keys[:, None, :] == block).astype(jnp.int32), axis=2)
    return codes, jnp.where(count > 0, upto - 1, CAP)


def shards(tile_values, tile_index, tile_count, user_prev, item_prev, day_prior):
    codes, last = sorted_codes(tile_index, tile_count)
    vmem = pl.BlockSpec(memory_space=pltpu.VMEM)
    smem = pl.BlockSpec(memory_space=pltpu.SMEM)
    block = (BLOCKS, R, TILE)
    users, items, days = pl.pallas_call(
        kernel,
        out_shape=(
            jax.ShapeDtypeStruct(user_prev.shape, F32),
            jax.ShapeDtypeStruct(item_prev.shape, F32),
            jax.ShapeDtypeStruct(day_prior.shape[::-1], F32),
        ),
        in_specs=[smem, smem, pl.BlockSpec(memory_space=pl.ANY), vmem, vmem, vmem],
        out_specs=(vmem, vmem, vmem),
        scratch_shapes=[
            pltpu.VMEM((CAP, TILE, TILE), BF16),
            pltpu.VMEM((CAP, TILE, TILE), BF16),
            pltpu.VMEM((CAP + 1, R, TILE), F32),
            pltpu.VMEM(block, F32),
            pltpu.VMEM(block, F32),
            pltpu.VMEM(block, BF16),
            pltpu.VMEM(block, BF16),
            pltpu.VMEM(block, F32),
            pltpu.VMEM(block, F32),
            pltpu.VMEM(block, F32),
            pltpu.VMEM((PASSES, *block), F32),
            pltpu.VMEM((PASSES, *block), F32),
            pltpu.VMEM(block, F32),
            pltpu.VMEM((1 + PASSES, 10, R // 2, 2 * R), F32),
            pltpu.VMEM((PASSES, 4, R // 2, 2 * R), F32),
            pltpu.VMEM((PASSES, 22, 16, TILE), F32),
            pltpu.VMEM((PASSES, 2, 22, 8, TILE), F32),
            pltpu.VMEM((PASSES, 6, 4, R, TILE), F32),
            pltpu.VMEM((PASSES, 16, R, TILE), F32),
            pltpu.VMEM((PASSES, 15, R, TILE), F32),
            pltpu.SemaphoreType.DMA,
            pltpu.SemaphoreType.DMA((COPIES,)),
            pltpu.SemaphoreType.DMA((COPIES,)),
        ],
        compiler_params=pltpu.CompilerParams(
            collective_id=0, has_side_effects=True, vmem_limit_bytes=60 * 1024 * 1024
        ),
    )(codes, last, tile_values, user_prev, item_prev, day_prior.T)
    return users, items, days.T


def solution(mesh):
    return jax.shard_map(
        shards,
        mesh=mesh,
        in_specs=(
            P(("au", "ia"), None, None),
            P(None, ("au", "ia")),
            P(("au", "ia")),
            P(None, "au"),
            P(None, "ia"),
            P(),
        ),
        out_specs=(P(None, "au"), P(None, "ia"), P()),
        check_vma=False,
    )
```

time: 298 us -> 179 us (0.60)
  Pallas kernels: 285 us -> 168 us
    pallas_call x1, Pallas kernels: 285 us -> 168 us  [shards(): pl.pallas_call(kernel, out_shape=(jax.ShapeDtypeStruct(user_prev.shape, F...]
where the time goes in v2:
time: 179 us
  Pallas kernels  168 us (94%)
  local copies, waits for them, and re-layouts  5.86 us (3%)
  other arithmetic  3.6 us (2%)
    pallas_call x1, Pallas kernels, shards(): pl.pallas_call(kernel, out_shape=(jax.ShapeDtypeStruct(user_prev.shape, F...  168 us
    unnamed x3, local copies, waits for them, and re-layouts  5.86 us

profile of v2, /device:TPU:1, one launch (start us, length us, event | category | flops | bytes accessed | tf_op | source)
XLA Modules:
  0.0 178.6 jit_solution(13236262368169855939)
XLA Ops:
  1.3 0.8 multiply_add_fusion
  2.1 0.7 iota_add_fusion
  2.8 0.5 fusion
  3.3 0.2 convert_reduce_fusion.2
  3.5 0.6 add_select_fusion.last
  4.1 0.8 select_reduce_fusion.codes
  4.9 167.9 %shard_map.85 = (f32[64,4096]{1,0:T(8,128)}, f32[64,4096]{1,0:T(8,128)}, f32[32,64]{1,0:T(8,128)}) custom-call(s32[3,256]{1,0:T(4,128)} %select_reduce_fusion.codes, s32[3,32]{1,0:T(4,128)} %add_select_fusion.last, bf16[256,128,128]{2,1,0:T(8,128)(2,1)} %tiles_hbm.1, f32[64,4096]{1,0:T(8,128)} %user_prior.1, f32[64,4096]{1,0:T(8,128)} %item_prior.1, ...), custom_call_target="tpu_custom_call" | custom-call | tf_op jit(solution)/shard_map/pallas_call | solution.py:500
  172.8 2.3 %copy.13 = f32[64,4096]{1,0:T(8,128)} copy(f32[64,4096]{1,0:T(8,128)} %get-tuple-element.18) | data formatting | bytes 2097152
  175.0 2.3 %copy.14 = f32[64,4096]{1,0:T(8,128)} copy(f32[64,4096]{1,0:T(8,128)} %get-tuple-element.19) | data formatting | bytes 2097152
  177.3 1.3 copy.15
  (2 shorter events, 0.0 us)

commit v3 on v2

--- a/solution.py
+++ b/solution.py
@@ -16,7 +16,7 @@
 EPSILON = 1e-06
 USER_ENTRIES = 64 * 131072
 ITEM_ENTRIES = 64 * 16384
-UNROLL = 32
+UNROLL = 64
 MESH = pl.DeviceIdType.MESH
 F32 = jnp.float32
 BF16 = jnp.bfloat16
@@ -67,7 +67,7 @@
         return copy
 
 
-COPIES = 7 + 7 * (PASSES - 1) + 7 + 3 * PASSES + PASSES * (19 + 19 + 19 + 6 + 6 + 1 + 15 + 15 + 1)
+COPIES = 7 + 7 * (PASSES - 1) + 7 + 3 * PASSES + PASSES * (19 + 19 + 19 + 12 + 12 + 4 + 15 + 15 + 4)
 
 
 def kernel(
@@ -141,68 +141,93 @@
             base += size
         result.append(value)
 
-    def reduce_ring(source, mine, along, width, got):
-        half = width // 2
-
-        def part(share, second):
-            return pl.ds(lax.rem(share, 4) * width + second * half, half)
-
-        far, right, left = mine + 2, mine + 1, mine + 3
-        c1 = copies.start(source.at[part(far, 0)], got.at[0], along(3))
-        c2 = copies.start(source.at[part(far, 1)], got.at[1], along(1))
-        c3 = copies.start(source.at[part(left, 1)], got.at[2], along(3))
-        c4 = copies.start(source.at[part(right, 0)], got.at[3], along(1))
+    def ring_part(share, piece):
+        return pl.ds(lax.rem(share, 4) * 8 + 2 * piece, 2)
+
+    def reduce_ring(source, part, got):
+        first, second = 2 * part, 2 * part + 1
+        far, right, left = x + 2, x + 1, x + 3
+        c1 = copies.start(source.at[ring_part(far, first)], got.at[0], along_x(3))
+        c2 = copies.start(source.at[ring_part(far, second)], got.at[1], along_x(1))
+        yield
+        c3 = copies.start(source.at[ring_part(left, second)], got.at[2], along_x(3))
+        c4 = copies.start(source.at[ring_part(right, first)], got.at[3], along_x(1))
         yield
         c1.wait()
-        source[part(left, 0)] = source[part(left, 0)] + got[0]
-        c5 = copies.start(source.at[part(left, 0)], got.at[4], along(3))
+        here = ring_part(left, first)
+        source[here] = source[here] + got[0]
+        c5 = copies.start(source.at[here], got.at[4], along_x(3))
         c2.wait()
-        source[part(right, 1)] = source[part(right, 1)] + got[1]
-        c6 = copies.start(source.at[part(right, 1)], got.at[5], along(1))
+        there = ring_part(right, second)
+        source[there] = source[there] + got[1]
+        c6 = copies.start(source.at[there], got.at[5], along_x(1))
         yield
         for copy in (c3, c4, c5, c6):
             copy.wait()
-        source[part(mine, 0)] = source[part(mine, 0)] + (got[4] + got[3])
-        source[part(mine, 1)] = source[part(mine, 1)] + (got[2] + got[5])
-
-    def gather_ring(source, mine, along, width):
-        half = width // 2
-
-        def part(share, second):
-            return source.at[pl.ds(lax.rem(share, 4) * width + second * half, half)]
-
-        left, right = mine + 3, mine + 1
-        c1 = copies.start(part(mine, 0), part(mine, 0), along(1))
-        c2 = copies.start(part(mine, 1), part(mine, 1), along(3))
-        c3 = copies.start(part(mine, 1), part(mine, 1), along(1))
-        c4 = copies.start(part(mine, 0), part(mine, 0), along(3))
+        mine = ring_part(x, first)
+        source[mine] = source[mine] + (got[4] + got[3])
+        mine = ring_part(x, second)
+        source[mine] = source[mine] + (got[2] + got[5])
+
+    def gather_ring(source, part):
+        def piece(share, which):
+            return source.at[ring_part(share, 2 * part + which)]
+
+        left, right = x + 3, x + 1
+        c1 = copies.start(piece(x, 0), piece(x, 0), along_x(1))
+        c2 = copies.start(piece(x, 1), piece(x, 1), along_x(3))
+        c3 = copies.start(piece(x, 1), piece(x, 1), along_x(1))
+        c4 = copies.start(piece(x, 0), piece(x, 0), along_x(3))
         yield
         c1.wait()
-        c5 = copies.start(part(left, 0), part(left, 0), along(1))
+        c5 = copies.start(piece(left, 0), piece(left, 0), along_x(1))
         c2.wait()
-        c6 = copies.start(part(right, 1), part(right, 1), along(3))
+        c6 = copies.start(piece(right, 1), piece(right, 1), along_x(3))
         yield
         for copy in (c3, c4, c5, c6):
             copy.wait()
 
-    def reduce_plane(source, base, got):
-        flying = [
-            copies.start(source.at[base + plane_of(step)], got.at[step - 1], along_yz(step))
-            for step in range(1, 16)
-        ]
+    def row_of(step):
+        return pl.ds(lax.rem(y + step, 4) * 4, 4)
+
+    def reduce_plane(source, got_core, got):
+        own, other = core * 16, 16 - core * 16
+        between = []
+        for row in (2, 1, 3, 0):
+            place = row_of(row)
+            between.append((row, copies.start(source.at[pl.ds(other + place.start, 4)], got_core.at[place], twin)))
+        yield
+        flying = []
+        for row, copy in between:
+            copy.wait()
+            place = row_of(row)
+            here = pl.ds(own + place.start, 4)
+            source[here] = source[here] + got_core[place]
+            for step in range(row * 4, row * 4 + 4):
+                if step:
+                    flying.append(copies.start(source.at[own + plane_of(step)], got.at[step - 1], along_yz(step)))
         yield
         for copy in flying:
             copy.wait()
-        total = source[base + plane]
+        total = source[own + plane]
         for step in range(15):
             total = total + got[step]
-        source[base + plane] = total
-
-    def gather_plane(source, base):
-        here = source.at[base + plane]
-        flying = [copies.start(here, here, along_yz(step)) for step in range(1, 16)]
-        yield
-        for copy in flying:
+        source[own + plane] = total
+
+    def gather_plane(source):
+        own = core * 16
+        here = source.at[own + plane]
+        flying = {step: copies.start(here, here, along_yz(step)) for row in (2, 1, 3, 0) for step in range(row * 4, row * 4 + 4) if step}
+        yield
+        between = []
+        for row in (0, 1, 3, 2):
+            for step in range(row * 4, row * 4 + 4):
+                if step:
+                    flying[step].wait()
+            place = source.at[pl.ds(own + row_of(4 - row).start, 4)]
+            between.append(copies.start(place, place, twin))
+        yield
+        for copy in between:
             copy.wait()
 
     def inverse(gram):
@@ -213,14 +238,28 @@
         matrix = gram / (trace / R) + 0.1 * diagonal[:, :R]
         matrix = jnp.concatenate([matrix, diagonal[:, :R]], axis=1)
 
+        place = rows[:8]
+
+        def wide(column):
+            return jnp.broadcast_to(column, (8, 2 * R))
+
         def eight(_, matrix):
+            top = matrix[:8]
+            columns = [wide(top[:, k : k + 1]) for k in range(8)]
             for k in range(8):
-                pivot = matrix[k : k + 1, k : k + 1]
-                row = matrix[k : k + 1, :] / pivot
-                column = matrix[:, k : k + 1] - jnp.where(rows[:, :1] == k, 1.0, 0.0)
-                matrix = matrix - column * row
-            matrix = jnp.concatenate([matrix[8:], matrix[:8]], axis=0)
-            return pltpu.roll(matrix, 2 * R - 8, 1)
+                share = 1.0 / columns[k][k : k + 1]
+                column = (columns[k] - jnp.where(place == k, 1.0, 0.0)) * share
+                top = top - column * top[k : k + 1]
+                for j in range(k + 1, 8):
+                    columns[j] = columns[j] - column * columns[j][k : k + 1]
+            rest = []
+            for begin in range(8, R, 8):
+                value = matrix[begin : begin + 8]
+                terms = [wide(value[:, k : k + 1]) * top[k : k + 1] for k in range(8)]
+                while len(terms) > 1:
+                    terms = [terms[k] + terms[k + 1] for k in range(0, len(terms), 2)]
+                rest.append(value - terms[0])
+            return pltpu.roll(jnp.concatenate(rest + [top], axis=0), 2 * R - 8, 1)
 
         return left_three(lax.fori_loop(0, R // 8, eight, matrix)[:, :R])
 
@@ -242,22 +281,22 @@
             acc = jnp.zeros((R, TILE), F32)
         return lax.fori_loop(begin // UNROLL, end // UNROLL, visit, acc)
 
-    def each_block(visit, by=4):
+    def each_block(visit, by=4, begin=0, count=BLOCKS):
         def some(step, carry):
             for k in range(by):
-                visit(step * by + k)
+                visit(begin + step * by + k)
             return carry
 
-        lax.fori_loop(0, BLOCKS // by, some, 0)
+        lax.fori_loop(0, count // by, some, 0)
 
     def columns(block):
         return pl.ds(pl.multiple_of(block * TILE, TILE), TILE)
 
-    def assemble(order, target):
+    def assemble(order, target, begin=0, count=BLOCKS):
         def visit(block):
             target[block] = running[last[order, block]]
 
-        each_block(visit, 8)
+        each_block(visit, 8, begin, count)
 
     def gram_of(source):
         def four(step, carry):
@@ -305,7 +344,7 @@
         for step in range(count):
             target[begin + step] = mm(inv, right_three(source[begin + step]))
 
-    def finish(target, target_half, t1, norm, out):
+    def finish(target, target_half, t1, norm, out, begin=0, count=BLOCKS):
         share = 1.0 / norm
 
         def visit(block):
@@ -315,7 +354,7 @@
             if out is not None:
                 out[:, columns(block)] = value
 
-        each_block(visit)
+        each_block(visit, 4, begin, count)
 
     def lay(block):
         value = user_prior[:, columns(block)]
@@ -327,7 +366,7 @@
 
     each_block(lay)
     running[CAP] = jnp.zeros((R, TILE), F32)
-    gu_part, gv_part = fold(gram_of(users)), fold(gram_of(items))
+    gu_part = fold(gram_of(users))
     day_rows = day_prior[...].T
     lanes = lax.broadcasted_iota(jnp.int32, (R, TILE), 1)
 
@@ -347,9 +386,6 @@
     for turn in range(PASSES):
         final = turn == PASSES - 1
 
-        gv_found = []
-        gv_job = total_over(("x",), gv_slots.at[turn], gv_part, gv_found)
-        next(gv_job)
         if turn == 0:
             tile_copy.wait()
 
@@ -375,6 +411,9 @@
         md_found = []
         md_job = total_over(("core", "x", "yz"), md_slots.at[turn], moments, md_found)
         next(md_job)
+        gv_found = []
+        gv_job = total_over(("x",), gv_slots.at[turn], fold(gram_of(items)), gv_found)
+        next(gv_job)
         next(md_job)
         if turn == 0:
             next(gu_job)
@@ -389,8 +428,8 @@
         else:
             drain(gv_job)
             gram_items = unfold(gv_found[0])
+            next(md_job)
             inv = inverse(gram_users * gram_items)
-            next(md_job)
         drain(md_job)
         moments = md_found[0]
         square = moments * moments
@@ -403,24 +442,31 @@
         days = mm(inv, right_three(moments + day_rows))
         for day in range(DAYS):
             spread[day] = jnp.broadcast_to(days[:, day : day + 1], (R, TILE))
+        if final:
+            day_out[...] = days.T
+
+        def user_product(tile, ub, ib, day):
+            return mm((items[ib] * spread[day]).astype(BF16), tile)
+
+        sweep(0, tiles_t, user_product)
+        assemble(0, mu)
+        parts = [reduce_ring(mu, part, urecv.at[turn, part]) for part in range(2)]
+        next(parts[0])
+        next(parts[0])
+        next(parts[1])
         high, low = halves(days)
         cross = mm(high, low, NT)
         gram_days = mm(high, high, NT) + (cross + mm(low, high, NT))
-        if final:
-            day_out[...] = days.T
-
-        def user_product(tile, ub, ib, day):
-            return mm((items[ib] * spread[day]).astype(BF16), tile)
-
-        sweep(0, tiles_t, user_product)
-        assemble(0, mu)
-        job = reduce_ring(mu, x, along_x, 8, urecv.at[turn])
-        next(job)
         inv = inverse(gram_items * gram_days)
-        drain(job)
-        apply(inv, mu, x * 8, 8, t1u.at[turn])
-        job = gather_ring(t1u.at[turn], x, along_x, 8)
-        next(job)
+        next(parts[0])
+        next(parts[1])
+        next(parts[1])
+        jobs = []
+        for part in range(2):
+            drain(parts[part])
+            apply(inv, mu, x * 8 + 4 * part, 4, t1u.at[turn])
+            jobs.append(gather_ring(t1u.at[turn], part))
+            next(jobs[part])
         scale_found = []
         scale_job = total_over(
             ("core", "yz", "x"), scale_slots.at[turn, 0], squares(mu, x * 8, 8), scale_found
@@ -428,10 +474,12 @@
         next(scale_job)
         next(scale_job)
         prior_part(inv, user_prior)
-        next(job)
+        next(jobs[0])
+        next(jobs[1])
         next(scale_job)
         drain(scale_job)
-        drain(job)
+        for job in jobs:
+            drain(job)
         finish(users, users_half, t1u.at[turn], scale_of(scale_found[0], USER_ENTRIES), user_out if final else None)
 
         gu_found = []
@@ -444,19 +492,17 @@
         acc = sweep(1, tiles, item_product, 0, CAP // 2)
         next(gu_job)
         sweep(1, tiles, item_product, CAP // 2, CAP, acc)
-        assemble(1, mi)
-        own, other = pl.ds(core * 16, 16), pl.ds(16 - core * 16, 16)
-        copy = copies.start(mi.at[other], irecv_core.at[turn], twin)
-        copy.wait()
-        mi[own] = mi[own] + irecv_core[turn]
-        job = reduce_plane(mi, core * 16, irecv.at[turn])
+        assemble(1, mi, 16 - core * 16, 16)
+        job = reduce_plane(mi, irecv_core.at[turn], irecv.at[turn])
+        next(job)
+        assemble(1, mi, core * 16, 16)
         next(job)
         drain(gu_job)
         gram_users = unfold(gu_found[0])
         inv = inverse(gram_users * gram_days)
         drain(job)
         apply(inv, mi, core * 16 + plane, 1, t1i.at[turn])
-        job = gather_plane(t1i.at[turn], core * 16)
+        job = gather_plane(t1i.at[turn])
         next(job)
         scale_found = []
         scale_job = total_over(
@@ -465,13 +511,13 @@
         next(scale_job)
         prior_part(inv, item_prior)
         next(scale_job)
+        next(job)
+        drain(scale_job)
+        norm = scale_of(scale_found[0], ITEM_ENTRIES)
+        out = item_out if final else None
+        finish(items, items_half, t1i.at[turn], norm, out, core * 16, 16)
         drain(job)
-        copy = copies.start(t1i.at[turn, own], t1i.at[turn, own], twin)
-        drain(scale_job)
-        copy.wait()
-        finish(items, items_half, t1i.at[turn], scale_of(scale_found[0], ITEM_ENTRIES), item_out if final else None)
-        if not final:
-            gv_part = fold(gram_of(items))
+        finish(items, items_half, t1i.at[turn], norm, out, 16 - core * 16, 16)
 
 
 def sorted_codes(tile_index, tile_count):
@@ -492,12 +538,34 @@
     return codes, jnp.where(count > 0, upto - 1, CAP)
 
 
+def copy_kernel(user_in, item_in, day_in, user_out, item_out, day_out, sem):
+    flying = [
+        pltpu.make_async_copy(source, target, sem.at[k])
+        for k, (source, target) in enumerate(((user_in, user_out), (item_in, item_out), (day_in, day_out)))
+    ]
+    for copy in flying:
+        copy.start()
+    for copy in flying:
+        copy.wait()
+
+
+def copied(arrays):
+    anywhere = pl.BlockSpec(memory_space=pl.ANY)
+    return pl.pallas_call(
+        copy_kernel,
+        out_shape=tuple(jax.ShapeDtypeStruct(one.shape, one.dtype) for one in arrays),
+        in_specs=[anywhere] * 3,
+        out_specs=(anywhere,) * 3,
+        scratch_shapes=[pltpu.SemaphoreType.DMA((3,))],
+    )(*arrays)
+
+
 def shards(tile_values, tile_index, tile_count, user_prev, item_prev, day_prior):
     codes, last = sorted_codes(tile_index, tile_count)
     vmem = pl.BlockSpec(memory_space=pltpu.VMEM)
     smem = pl.BlockSpec(memory_space=pltpu.SMEM)
     block = (BLOCKS, R, TILE)
-    users, items, days = pl.pallas_call(
+    results = pl.pallas_call(
         kernel,
         out_shape=(
             jax.ShapeDtypeStruct(user_prev.shape, F32),
@@ -524,7 +592,7 @@
             pltpu.VMEM((PASSES, 4, R // 2, 2 * R), F32),
             pltpu.VMEM((PASSES, 22, 16, TILE), F32),
             pltpu.VMEM((PASSES, 2, 22, 8, TILE), F32),
-            pltpu.VMEM((PASSES, 6, 4, R, TILE), F32),
+            pltpu.VMEM((PASSES, 2, 6, 2, R, TILE), F32),
             pltpu.VMEM((PASSES, 16, R, TILE), F32),
             pltpu.VMEM((PASSES, 15, R, TILE), F32),
             pltpu.SemaphoreType.DMA,
@@ -535,6 +603,7 @@
             collective_id=0, has_side_effects=True, vmem_limit_bytes=60 * 1024 * 1024
         ),
     )(codes, last, tile_values, user_prev, item_prev, day_prior.T)
+    users, items, days = copied(results)
     return users, items, days.T
 
 

time: 179 us -> 223 us (1.25)
  Pallas kernels: 168 us -> 218 us
  local copies, waits for them, and re-layouts: 5.86 us -> 0 us
    pallas_call x0 -> x1, Pallas kernels: none -> 65.2 us  [copied(): pl.pallas_call(copy_kernel, out_shape=tuple((jax.ShapeDtypeStruct(one.sha...]
    pallas_call x1, Pallas kernels: 168 us -> 153 us  [shards(): pl.pallas_call(kernel, out_shape=(jax.ShapeDtypeStruct(user_prev.shape, F...]
    unnamed x3 -> x0, local copies, waits for them, and re-layouts: 5.86 us -> none
where the time goes in v3:
time: 223 us
  Pallas kernels  218 us (98%)
  other arithmetic  3.6 us (2%)
    pallas_call x1, Pallas kernels, shards(): pl.pallas_call(kernel, out_shape=(jax.ShapeDtypeStruct(user_prev.shape, F...  153 us
    pallas_call x1, Pallas kernels, copied(): pl.pallas_call(copy_kernel, out_shape=tuple((jax.ShapeDtypeStruct(one.sha...  65.2 us

profile of v3, /device:TPU:1, one launch (start us, length us, event | category | flops | bytes accessed | tf_op | source)
XLA Modules:
  0.0 222.6 jit_solution(15280515687668386934)
XLA Ops:
  1.3 0.8 multiply_add_fusion
  2.1 0.7 iota_add_fusion
  2.8 0.5 fusion
  3.3 0.2 convert_reduce_fusion.2
  3.5 0.6 add_select_fusion.last
  4.1 0.8 select_reduce_fusion.codes
  4.9 152.5 %shard_map.85 = (f32[64,4096]{1,0:T(8,128)}, f32[64,4096]{1,0:T(8,128)}, f32[32,64]{1,0:T(8,128)}) custom-call(s32[3,256]{1,0:T(4,128)} %select_reduce_fusion.codes, s32[3,32]{1,0:T(4,128)} %add_select_fusion.last, bf16[256,128,128]{2,1,0:T(8,128)(2,1)} %tiles_hbm.1, f32[64,4096]{1,0:T(8,128)} %user_prior.1, f32[64,4096]{1,0:T(8,128)} %item_prior.1, ...), custom_call_target="tpu_custom_call" | custom-call | tf_op jit(solution)/shard_map/pallas_call | solution.py:568
  157.4 65.2 %shard_map.86 = (f32[64,4096]{1,0:T(8,128)}, f32[64,4096]{1,0:T(8,128)}, f32[32,64]{1,0:T(8,128)}) custom-call(f32[64,4096]{1,0:T(8,128)} %get-tuple-element.9.user_in, f32[64,4096]{1,0:T(8,128)} %get-tuple-element.10.item_in, f32[32,64]{1,0:T(8,128)} %get-tuple-element.11.day_in), custom_call_target="tpu_custom_call" | custom-call | tf_op jit(solution)/shard_map/pallas_call | solution.py:554
  (2 shorter events, 0.0 us)

commit v4 on v3

--- a/solution.py
+++ b/solution.py
@@ -49,34 +49,72 @@
         pass
 
 
-class Copies:
+class Group:
+    def __init__(self, sems):
+        self.send, self.recv = sems
+
+    def start(self, source, target, device):
+        pltpu.make_async_remote_copy(
+            src_ref=source,
+            dst_ref=target,
+            send_sem=self.send,
+            recv_sem=self.recv,
+            device_id=device,
+            device_id_type=MESH,
+        ).start()
+
+    def wait(self, all_of_it):
+        pltpu.make_async_copy(all_of_it, all_of_it, self.recv).wait()
+        pltpu.make_async_copy(all_of_it, all_of_it, self.send).wait()
+
+
+class Groups:
     def __init__(self, send, recv):
         self.send, self.recv, self.used = send, recv, 0
 
-    def start(self, source, target, device):
-        copy = pltpu.make_async_remote_copy(
-            src_ref=source,
-            dst_ref=target,
-            send_sem=self.send.at[self.used],
-            recv_sem=self.recv.at[self.used],
-            device_id=device,
-            device_id_type=MESH,
-        )
+    def new(self):
         self.used += 1
-        copy.start()
-        return copy
-
-
-COPIES = 7 + 7 * (PASSES - 1) + 7 + 3 * PASSES + PASSES * (19 + 19 + 19 + 12 + 12 + 4 + 15 + 15 + 4)
+        return Group((self.send.at[self.used - 1], self.recv.at[self.used - 1]))
+
+
+GROUPS = 3 + PASSES * (3 + 1 + 3 + 3 + 3 + 4 + 4 + 4 + 1 + 4 + 1)
+
+
+def order_slots(index, live, codes, last):
+    slot = lax.broadcasted_iota(jnp.int32, (8, CAP), 1)
+    rows = jnp.concatenate([index[...], jnp.zeros((5, CAP), jnp.int32)], axis=0)
+    keys = jnp.where(slot < live, rows, BLOCKS)
+    unique = keys * CAP + slot
+    unique_down = unique.T
+    code = slot[:1] + rows[:1] * 256 + rows[1:2] * 8192 + rows[2:3] * 262144
+    ranks = [
+        jnp.sum(jnp.where(unique_down[:, k : k + 1] < unique[k : k + 1], 1, 0), axis=0, keepdims=True)
+        for k in range(3)
+    ]
+    down = jnp.concatenate(ranks + [code, slot[:4]], axis=0).T
+    keys_down = keys.T
+    place = lax.broadcasted_iota(jnp.int32, (CAP, CAP), 1)
+    block = lax.broadcasted_iota(jnp.int32, (CAP, TILE), 1)
+    for k in range(3):
+        chosen = jnp.where(down[:, k : k + 1] == place, down[:, 3:4], 0)
+        chosen = jnp.sum(chosen, axis=0, keepdims=True)
+        key = jnp.where(slot[:1] < live, (chosen >> (8 + 5 * k)) & 31, BLOCKS)
+        starts = (slot[:1] == 0) | (key != pltpu.roll(key, 1, 1))
+        codes[k : k + 1, :] = chosen + jnp.where(starts, 1 << 23, 0)
+        upto = jnp.sum(jnp.where(keys_down[:, k : k + 1] <= block, 1, 0), axis=0, keepdims=True)
+        count = jnp.sum(jnp.where(keys_down[:, k : k + 1] == block, 1, 0), axis=0, keepdims=True)
+        last[k : k + 1, :] = jnp.where(count > 0, upto - 1, CAP)
 
 
 def kernel(
-    codes, last, tiles_hbm, user_prior, item_prior, day_prior,
+    index, live_count, tiles_hbm, user_hbm, item_hbm, day_prior,
     user_out, item_out, day_out,
+    user_prior, item_prior,
     tiles, tiles_t, running, users, items, users_half, items_half, spread,
     mu, mi, t1u, t1i, t2,
     gu_slots, gv_slots, md_slots, scale_slots, urecv, irecv_core, irecv,
-    tile_sem, send, recv,
+    codes_made, last_made, codes, last,
+    tile_sem, prior_sem, out_sem, order_sem, send, recv,
 ):
     au = lax.axis_index("au")
     x = lax.axis_index("ia")
@@ -114,9 +152,15 @@
         "yz": (16, plane, along_yz),
     }
 
-    copies = Copies(send, recv)
+    groups = Groups(send, recv)
 
     tile_copy = pltpu.make_async_copy(tiles_hbm, tiles, tile_sem)
+    prior_copies = [
+        pltpu.make_async_copy(user_hbm, user_prior, prior_sem.at[0]),
+        pltpu.make_async_copy(item_hbm, item_prior, prior_sem.at[1]),
+    ]
+    for copy in prior_copies:
+        copy.start()
     tile_copy.start()
 
     barrier = pltpu.get_barrier_semaphore()
@@ -130,10 +174,11 @@
             size, mine, along = kinds[stage]
             here = where.at[base + mine]
             where[base + mine] = value
-            flying = [copies.start(here, here, along(step)) for step in range(1, size)]
+            group = groups.new()
+            for step in range(1, size):
+                group.start(here, here, along(step))
             yield
-            for copy in flying:
-                copy.wait()
+            group.wait(where.at[pl.ds(base, size - 1)])
             terms = [where[base + place] for place in range(size)]
             while len(terms) > 1:
                 terms = [terms[k] + terms[k + 1] for k in range(0, len(terms), 2)]
@@ -147,23 +192,22 @@
     def reduce_ring(source, part, got):
         first, second = 2 * part, 2 * part + 1
         far, right, left = x + 2, x + 1, x + 3
-        c1 = copies.start(source.at[ring_part(far, first)], got.at[0], along_x(3))
-        c2 = copies.start(source.at[ring_part(far, second)], got.at[1], along_x(1))
-        yield
-        c3 = copies.start(source.at[ring_part(left, second)], got.at[2], along_x(3))
-        c4 = copies.start(source.at[ring_part(right, first)], got.at[3], along_x(1))
-        yield
-        c1.wait()
+        distant, close = groups.new(), groups.new()
+        distant.start(source.at[ring_part(far, first)], got.at[0], along_x(3))
+        distant.start(source.at[ring_part(far, second)], got.at[1], along_x(1))
+        yield
+        close.start(source.at[ring_part(left, second)], got.at[2], along_x(3))
+        close.start(source.at[ring_part(right, first)], got.at[3], along_x(1))
+        yield
+        distant.wait(got.at[pl.ds(0, 2)])
         here = ring_part(left, first)
         source[here] = source[here] + got[0]
-        c5 = copies.start(source.at[here], got.at[4], along_x(3))
-        c2.wait()
+        close.start(source.at[here], got.at[4], along_x(3))
         there = ring_part(right, second)
         source[there] = source[there] + got[1]
-        c6 = copies.start(source.at[there], got.at[5], along_x(1))
-        yield
-        for copy in (c3, c4, c5, c6):
-            copy.wait()
+        close.start(source.at[there], got.at[5], along_x(1))
+        yield
+        close.wait(got.at[pl.ds(2, 4)])
         mine = ring_part(x, first)
         source[mine] = source[mine] + (got[4] + got[3])
         mine = ring_part(x, second)
@@ -174,18 +218,17 @@
             return source.at[ring_part(share, 2 * part + which)]
 
         left, right = x + 3, x + 1
-        c1 = copies.start(piece(x, 0), piece(x, 0), along_x(1))
-        c2 = copies.start(piece(x, 1), piece(x, 1), along_x(3))
-        c3 = copies.start(piece(x, 1), piece(x, 1), along_x(1))
-        c4 = copies.start(piece(x, 0), piece(x, 0), along_x(3))
-        yield
-        c1.wait()
-        c5 = copies.start(piece(left, 0), piece(left, 0), along_x(1))
-        c2.wait()
-        c6 = copies.start(piece(right, 1), piece(right, 1), along_x(3))
-        yield
-        for copy in (c3, c4, c5, c6):
-            copy.wait()
+        onward, rest = groups.new(), groups.new()
+        onward.start(piece(x, 0), piece(x, 0), along_x(1))
+        onward.start(piece(x, 1), piece(x, 1), along_x(3))
+        rest.start(piece(x, 1), piece(x, 1), along_x(1))
+        rest.start(piece(x, 0), piece(x, 0), along_x(3))
+        yield
+        onward.wait(source.at[pl.ds(0, 4)])
+        rest.start(piece(left, 0), piece(left, 0), along_x(1))
+        rest.start(piece(right, 1), piece(right, 1), along_x(3))
+        yield
+        rest.wait(source.at[pl.ds(0, 8)])
 
     def row_of(step):
         return pl.ds(lax.rem(y + step, 4) * 4, 4)
@@ -195,20 +238,21 @@
         between = []
         for row in (2, 1, 3, 0):
             place = row_of(row)
-            between.append((row, copies.start(source.at[pl.ds(other + place.start, 4)], got_core.at[place], twin)))
-        yield
-        flying = []
-        for row, copy in between:
-            copy.wait()
+            group = groups.new()
+            group.start(source.at[pl.ds(other + place.start, 4)], got_core.at[place], twin)
+            between.append((row, group))
+        yield
+        flying = groups.new()
+        for row, group in between:
             place = row_of(row)
+            group.wait(got_core.at[place])
             here = pl.ds(own + place.start, 4)
             source[here] = source[here] + got_core[place]
             for step in range(row * 4, row * 4 + 4):
                 if step:
-                    flying.append(copies.start(source.at[own + plane_of(step)], got.at[step - 1], along_yz(step)))
-        yield
-        for copy in flying:
-            copy.wait()
+                    flying.start(source.at[own + plane_of(step)], got.at[step - 1], along_yz(step))
+        yield
+        flying.wait(got)
         total = source[own + plane]
         for step in range(15):
             total = total + got[step]
@@ -217,18 +261,19 @@
     def gather_plane(source):
         own = core * 16
         here = source.at[own + plane]
-        flying = {step: copies.start(here, here, along_yz(step)) for row in (2, 1, 3, 0) for step in range(row * 4, row * 4 + 4) if step}
-        yield
-        between = []
-        for row in (0, 1, 3, 2):
+        flying = {row: groups.new() for row in range(4)}
+        for row in (2, 1, 3, 0):
             for step in range(row * 4, row * 4 + 4):
                 if step:
-                    flying[step].wait()
+                    flying[row].start(here, here, along_yz(step))
+        yield
+        between = groups.new()
+        for row in (0, 1, 3, 2):
+            flying[row].wait(source.at[pl.ds(0, 4 if row else 3)])
             place = source.at[pl.ds(own + row_of(4 - row).start, 4)]
-            between.append(copies.start(place, place, twin))
-        yield
-        for copy in between:
-            copy.wait()
+            between.start(place, place, twin)
+        yield
+        between.wait(source.at[pl.ds(0, 16)])
 
     def inverse(gram):
         rows = lax.broadcasted_iota(jnp.int32, (R, 2 * R), 0)
@@ -344,7 +389,7 @@
         for step in range(count):
             target[begin + step] = mm(inv, right_three(source[begin + step]))
 
-    def finish(target, target_half, t1, norm, out, begin=0, count=BLOCKS):
+    def finish(target, target_half, t1, norm, out=None, begin=0, count=BLOCKS):
         share = 1.0 / norm
 
         def visit(block):
@@ -355,6 +400,12 @@
                 out[:, columns(block)] = value
 
         each_block(visit, 4, begin, count)
+
+    order_slots(index, live_count[0], codes_made, last_made)
+    codes_copy = pltpu.make_async_copy(codes_made, codes, order_sem.at[0])
+    last_copy = pltpu.make_async_copy(last_made, last, order_sem.at[1])
+    codes_copy.start()
+    last_copy.start()
 
     def lay(block):
         value = user_prior[:, columns(block)]
@@ -364,6 +415,8 @@
         items[block] = value
         items_half[block] = value.astype(BF16)
 
+    for copy in prior_copies:
+        copy.wait()
     each_block(lay)
     running[CAP] = jnp.zeros((R, TILE), F32)
     gu_part = fold(gram_of(users))
@@ -378,24 +431,21 @@
 
         lax.fori_loop(begin // 16, end // 16, visit, 0)
 
-    pl.semaphore_wait(barrier, len(peers))
     gu_found = []
     gu_job = total_over(("core", "y", "z"), gu_slots.at[0], gu_part, gu_found)
-    next(gu_job)
 
     for turn in range(PASSES):
         final = turn == PASSES - 1
 
         if turn == 0:
             tile_copy.wait()
+            codes_copy.wait()
+            last_copy.wait()
 
         def day_product(tile, ub, ib, day):
             return mm(users_half[ub], tile) * items_half[ib].astype(F32)
 
-        acc = sweep(2, tiles, day_product, 0, CAP // 2)
-        if turn == 0:
-            next(gu_job)
-        sweep(2, tiles, day_product, CAP // 2, CAP, acc)
+        sweep(2, tiles, day_product)
 
         def day_sums(step, total):
             for k in range(8):
@@ -410,26 +460,32 @@
         )
         md_found = []
         md_job = total_over(("core", "x", "yz"), md_slots.at[turn], moments, md_found)
-        next(md_job)
         gv_found = []
-        gv_job = total_over(("x",), gv_slots.at[turn], fold(gram_of(items)), gv_found)
+        if turn == 0:
+            gv_part = fold(gram_of(items))
+            pl.semaphore_wait(barrier, len(peers))
+            next(gu_job)
+            next(md_job)
+        else:
+            next(md_job)
+            gv_part = fold(gram_of(items))
+        gv_job = total_over(("x",), gv_slots.at[turn], gv_part, gv_found)
         next(gv_job)
+        if turn == 0:
+            next(gu_job)
         next(md_job)
         if turn == 0:
+            transpose_tiles(0, CAP // 2)
             next(gu_job)
-            transpose_tiles(0, CAP // 2)
             next(md_job)
             transpose_tiles(CAP // 2, CAP)
             drain(gu_job)
             gram_users = unfold(gu_found[0])
-            drain(gv_job)
-            gram_items = unfold(gv_found[0])
-            inv = inverse(gram_users * gram_items)
-        else:
-            drain(gv_job)
-            gram_items = unfold(gv_found[0])
+        drain(gv_job)
+        gram_items = unfold(gv_found[0])
+        if turn:
             next(md_job)
-            inv = inverse(gram_users * gram_items)
+        inv = inverse(gram_users * gram_items)
         drain(md_job)
         moments = md_found[0]
         square = moments * moments
@@ -480,7 +536,11 @@
         drain(scale_job)
         for job in jobs:
             drain(job)
-        finish(users, users_half, t1u.at[turn], scale_of(scale_found[0], USER_ENTRIES), user_out if final else None)
+        norm = scale_of(scale_found[0], USER_ENTRIES)
+        finish(users, users_half, t1u.at[turn], norm, user_prior if final else None)
+        if final:
+            user_copy = pltpu.make_async_copy(user_prior, user_out, out_sem.at[0])
+            user_copy.start()
 
         gu_found = []
         gu_job = total_over(("core", "y", "z"), gu_slots.at[1 + turn], fold(gram_of(users)), gu_found)
@@ -501,41 +561,35 @@
         gram_users = unfold(gu_found[0])
         inv = inverse(gram_users * gram_days)
         drain(job)
+        scale_found = []
+        scale_job = total_over(
+            ("yz", "core", "x"), scale_slots.at[turn, 1], squares(mi, core * 16 + plane, 1), scale_found
+        )
+        next(scale_job)
         apply(inv, mi, core * 16 + plane, 1, t1i.at[turn])
         job = gather_plane(t1i.at[turn])
         next(job)
-        scale_found = []
-        scale_job = total_over(
-            ("x", "yz", "core"), scale_slots.at[turn, 1], squares(mi, core * 16 + plane, 1), scale_found
-        )
+        prior_part(inv, item_prior)
         next(scale_job)
-        prior_part(inv, item_prior)
         next(scale_job)
         next(job)
         drain(scale_job)
         norm = scale_of(scale_found[0], ITEM_ENTRIES)
-        out = item_out if final else None
-        finish(items, items_half, t1i.at[turn], norm, out, core * 16, 16)
-        drain(job)
-        finish(items, items_half, t1i.at[turn], norm, out, 16 - core * 16, 16)
-
-
-def sorted_codes(tile_index, tile_count):
-    slot = jnp.arange(CAP, dtype=jnp.int32)
-    live = slot < tile_count[0]
-    keys = jnp.where(live[None, :], tile_index, BLOCKS)
-    unique = keys * CAP + slot[None, :]
-    before = unique[:, None, :] < unique[:, :, None]
-    same = keys[:, None, :] == keys[:, :, None]
-    rank = jnp.sum(before.astype(jnp.int32), axis=2)
-    follows = jnp.sum((before & same).astype(jnp.int32), axis=2) > 0
-    code = slot + tile_index[0] * 256 + tile_index[1] * 8192 + tile_index[2] * 262144
-    code = code[None, :] + jnp.where(follows, 0, 1 << 23)
-    codes = jnp.sum(jnp.where(rank[:, None, :] == slot[None, :, None], code[:, None, :], 0), axis=2)
-    block = jnp.arange(BLOCKS, dtype=jnp.int32)[None, :, None]
-    upto = jnp.sum((keys[:, None, :] <= block).astype(jnp.int32), axis=2)
-    count = jnp.sum((keys[:, None, :] == block).astype(jnp.int32), axis=2)
-    return codes, jnp.where(count > 0, upto - 1, CAP)
+        out = item_prior if final else None
+        item_copies = []
+        for part, begin in enumerate((core * 16, 16 - core * 16)):
+            if part == 1:
+                drain(job)
+            finish(items, items_half, t1i.at[turn], norm, out, begin, 16)
+            if final:
+                half = pl.ds(pl.multiple_of(begin * TILE, 16 * TILE), 16 * TILE)
+                copy = pltpu.make_async_copy(item_prior.at[:, half], item_out.at[:, half], out_sem.at[1 + part])
+                copy.start()
+                item_copies.append(copy)
+
+    user_copy.wait()
+    for copy in item_copies:
+        copy.wait()
 
 
 def copy_kernel(user_in, item_in, day_in, user_out, item_out, day_out, sem):
@@ -550,20 +604,19 @@
 
 
 def copied(arrays):
-    anywhere = pl.BlockSpec(memory_space=pl.ANY)
     return pl.pallas_call(
         copy_kernel,
         out_shape=tuple(jax.ShapeDtypeStruct(one.shape, one.dtype) for one in arrays),
-        in_specs=[anywhere] * 3,
-        out_specs=(anywhere,) * 3,
+        in_specs=[pl.BlockSpec(memory_space=pltpu.VMEM)] * 3,
+        out_specs=(pl.BlockSpec(memory_space=pl.ANY),) * 3,
         scratch_shapes=[pltpu.SemaphoreType.DMA((3,))],
     )(*arrays)
 
 
 def shards(tile_values, tile_index, tile_count, user_prev, item_prev, day_prior):
-    codes, last = sorted_codes(tile_index, tile_count)
     vmem = pl.BlockSpec(memory_space=pltpu.VMEM)
     smem = pl.BlockSpec(memory_space=pltpu.SMEM)
+    anywhere = pl.BlockSpec(memory_space=pl.ANY)
     block = (BLOCKS, R, TILE)
     results = pl.pallas_call(
         kernel,
@@ -572,9 +625,11 @@
             jax.ShapeDtypeStruct(item_prev.shape, F32),
             jax.ShapeDtypeStruct(day_prior.shape[::-1], F32),
         ),
-        in_specs=[smem, smem, pl.BlockSpec(memory_space=pl.ANY), vmem, vmem, vmem],
-        out_specs=(vmem, vmem, vmem),
+        in_specs=[vmem, smem, anywhere, anywhere, anywhere, vmem],
+        out_specs=(anywhere, anywhere, vmem),
         scratch_shapes=[
+            pltpu.VMEM(user_prev.shape, F32),
+            pltpu.VMEM(item_prev.shape, F32),
             pltpu.VMEM((CAP, TILE, TILE), BF16),
             pltpu.VMEM((CAP, TILE, TILE), BF16),
             pltpu.VMEM((CAP + 1, R, TILE), F32),
@@ -595,14 +650,21 @@
             pltpu.VMEM((PASSES, 2, 6, 2, R, TILE), F32),
             pltpu.VMEM((PASSES, 16, R, TILE), F32),
             pltpu.VMEM((PASSES, 15, R, TILE), F32),
+            pltpu.VMEM((8, CAP), jnp.int32),
+            pltpu.VMEM((8, TILE), jnp.int32),
+            pltpu.SMEM((8, CAP), jnp.int32),
+            pltpu.SMEM((8, TILE), jnp.int32),
             pltpu.SemaphoreType.DMA,
-            pltpu.SemaphoreType.DMA((COPIES,)),
-            pltpu.SemaphoreType.DMA((COPIES,)),
+            pltpu.SemaphoreType.DMA((2,)),
+            pltpu.SemaphoreType.DMA((3,)),
+            pltpu.SemaphoreType.DMA((2,)),
+            pltpu.SemaphoreType.DMA((GROUPS,)),
+            pltpu.SemaphoreType.DMA((GROUPS,)),
         ],
         compiler_params=pltpu.CompilerParams(
-            collective_id=0, has_side_effects=True, vmem_limit_bytes=60 * 1024 * 1024
+            collective_id=0, has_side_effects=True, vmem_limit_bytes=63 * 1024 * 1024
         ),
-    )(codes, last, tile_values, user_prev, item_prev, day_prior.T)
+    )(tile_index, tile_count, tile_values, user_prev, item_prev, day_prior.T)
     users, items, days = copied(results)
     return users, items, days.T
 

time: 223 us -> 152 us (0.68)
  Pallas kernels: 218 us -> 150 us
  other arithmetic: 3.6 us -> 0 us
    pallas_call x1, Pallas kernels: 65.2 us -> 2.89 us  [copied(): pl.pallas_call(copy_kernel, out_shape=tuple((jax.ShapeDtypeStruct(one.sha...]
    pallas_call x1, Pallas kernels: 153 us -> 147 us  [shards(): pl.pallas_call(kernel, out_shape=(jax.ShapeDtypeStruct(user_prev.shape, F...]
where the time goes in v4:
time: 152 us
  Pallas kernels  150 us (99%)
    pallas_call x1, Pallas kernels, shards(): pl.pallas_call(kernel, out_shape=(jax.ShapeDtypeStruct(user_prev.shape, F...  147 us

profile of v4, /device:TPU:1, one launch (start us, length us, event | category | flops | bytes accessed | tf_op | source)
XLA Modules:
  0.0 151.6 jit_solution(6735235677592244824)
XLA Ops:
  1.3 147.5 %shard_map.85 = (f32[64,4096]{1,0:T(8,128)}, f32[64,4096]{1,0:T(8,128)}, f32[32,64]{1,0:T(8,128)}) custom-call(s32[3,256]{1,0:T(4,128)} %index.1, s32[1]{0:T(128)S(6)} %copy.9.live_count, bf16[256,128,128]{2,1,0:T(8,128)(2,1)} %tiles_hbm.1, f32[64,4096]{1,0:T(8,128)} %user_hbm.1, f32[64,4096]{1,0:T(8,128)} %item_hbm.1, f32[32,64]{1,0:T(8,128)} %bitcast.2), custom_call_target="tpu_custom_call" | custom-call | tf_op jit(solution)/shard_map/pallas_call | solution.py:621
  148.8 2.9 %shard_map.86 = (f32[64,4096]{1,0:T(8,128)}, f32[64,4096]{1,0:T(8,128)}, f32[32,64]{1,0:T(8,128)}) custom-call(f32[64,4096]{1,0:T(8,128)} %get-tuple-element.9.user_in, f32[64,4096]{1,0:T(8,128)} %get-tuple-element.10.item_in, f32[32,64]{1,0:T(8,128)} %get-tuple-element.11.day_in), custom_call_target="tpu_custom_call" | custom-call | tf_op jit(solution)/shard_map/pallas_call | solution.py:607

commit v5 on v4

--- a/solution.py
+++ b/solution.py
@@ -77,7 +77,7 @@
         return Group((self.send.at[self.used - 1], self.recv.at[self.used - 1]))
 
 
-GROUPS = 3 + PASSES * (3 + 1 + 3 + 3 + 3 + 4 + 4 + 4 + 1 + 4 + 1)
+GROUPS = 2 + PASSES * (3 + 1 + 3 + 3 + 3 + 4 + 4 + 4 + 1 + 4 + 1)
 
 
 def order_slots(index, live, codes, last):
@@ -137,6 +137,8 @@
     def along_z(step):
         return (at(y, lax.rem(z + step, 4), core), x)
 
+    far_first = (2, 1, 3, 0)
+
     def along_yz(step):
         yy, zz = lax.rem(y + step // 4, 4), lax.rem(z + step % 4, 4)
         return (at(yy, zz, core), x)
@@ -150,6 +152,15 @@
         "y": (4, y, along_y),
         "z": (4, z, along_z),
         "yz": (16, plane, along_yz),
+    }
+
+    def distance(step):
+        return (0, 1, 2, 1)[step // 4] + (0, 1, 2, 1)[step % 4]
+
+    orders = {
+        2: (1,),
+        4: (2, 1, 3),
+        16: sorted(range(1, 16), key=lambda step: -distance(step)),
     }
 
     groups = Groups(send, recv)
@@ -175,7 +186,7 @@
             here = where.at[base + mine]
             where[base + mine] = value
             group = groups.new()
-            for step in range(1, size):
+            for step in orders[size]:
                 group.start(here, here, along(step))
             yield
             group.wait(where.at[pl.ds(base, size - 1)])
@@ -236,7 +247,7 @@
     def reduce_plane(source, got_core, got):
         own, other = core * 16, 16 - core * 16
         between = []
-        for row in (2, 1, 3, 0):
+        for row in far_first:
             place = row_of(row)
             group = groups.new()
             group.start(source.at[pl.ds(other + place.start, 4)], got_core.at[place], twin)
@@ -248,7 +259,7 @@
             group.wait(got_core.at[place])
             here = pl.ds(own + place.start, 4)
             source[here] = source[here] + got_core[place]
-            for step in range(row * 4, row * 4 + 4):
+            for step in (row * 4 + further for further in far_first):
                 if step:
                     flying.start(source.at[own + plane_of(step)], got.at[step - 1], along_yz(step))
         yield
@@ -262,8 +273,8 @@
         own = core * 16
         here = source.at[own + plane]
         flying = {row: groups.new() for row in range(4)}
-        for row in (2, 1, 3, 0):
-            for step in range(row * 4, row * 4 + 4):
+        for row in far_first:
+            for step in (row * 4 + further for further in far_first):
                 if step:
                     flying[row].start(here, here, along_yz(step))
         yield
@@ -308,23 +319,33 @@
 
         return left_three(lax.fori_loop(0, R // 8, eight, matrix)[:, :R])
 
-    def sweep(order, source, product, begin=0, end=CAP, acc=None):
+    def place_of(order, place):
+        code = codes[order, place]
+        keep = (1 - (code >> 23)).astype(F32)
+        return code & 255, (code >> 8) & 31, (code >> 13) & 31, (code >> 18) & 31, keep
+
+    def sweep(order, product, begin=0, end=CAP, acc=None):
         def visit(turn, acc):
             for k in range(UNROLL):
                 place = turn * UNROLL + k
-                code = codes[order, place]
-                slot = code & 255
-                ub = (code >> 8) & 31
-                ib = (code >> 13) & 31
-                day = (code >> 18) & 31
-                keep = (1 - (code >> 23)).astype(F32)
-                acc = acc * keep + product(source[slot], ub, ib, day)
+                *chosen, keep = place_of(order, place)
+                acc = acc * keep + product(place, *chosen)
                 running[place] = acc
             return acc
 
         if acc is None:
             acc = jnp.zeros((R, TILE), F32)
         return lax.fori_loop(begin // UNROLL, end // UNROLL, visit, acc)
+
+    def day_partials(begin, end):
+        def visit(turn, carry):
+            for k in range(UNROLL):
+                place = turn * UNROLL + k
+                slot, ub, _, _, _ = place_of(2, place)
+                running[place] = mm(users_half[ub], tiles[slot])
+            return carry
+
+        lax.fori_loop(begin // UNROLL, end // UNROLL, visit, 0)
 
     def each_block(visit, by=4, begin=0, count=BLOCKS):
         def some(step, carry):
@@ -432,7 +453,7 @@
         lax.fori_loop(begin // 16, end // 16, visit, 0)
 
     gu_found = []
-    gu_job = total_over(("core", "y", "z"), gu_slots.at[0], gu_part, gu_found)
+    gu_job = total_over(("core", "yz"), gu_slots.at[0], gu_part, gu_found)
 
     for turn in range(PASSES):
         final = turn == PASSES - 1
@@ -442,10 +463,19 @@
             codes_copy.wait()
             last_copy.wait()
 
-        def day_product(tile, ub, ib, day):
-            return mm(users_half[ub], tile) * items_half[ib].astype(F32)
-
-        sweep(2, tiles, day_product)
+        def day_product(place, slot, ub, ib, day):
+            if turn == 0:
+                return mm(users_half[ub], tiles[slot]) * items_half[ib].astype(F32)
+            return running[place] * items_half[ib].astype(F32)
+
+        if turn == 0:
+            acc = sweep(2, day_product, 0, CAP // 2)
+            pl.semaphore_wait(barrier, len(peers))
+            next(gu_job)
+            sweep(2, day_product, CAP // 2, CAP, acc)
+            next(gu_job)
+        else:
+            sweep(2, day_product)
 
         def day_sums(step, total):
             for k in range(8):
@@ -460,51 +490,38 @@
         )
         md_found = []
         md_job = total_over(("core", "x", "yz"), md_slots.at[turn], moments, md_found)
+        next(md_job)
         gv_found = []
-        if turn == 0:
-            gv_part = fold(gram_of(items))
-            pl.semaphore_wait(barrier, len(peers))
-            next(gu_job)
-            next(md_job)
-        else:
-            next(md_job)
-            gv_part = fold(gram_of(items))
-        gv_job = total_over(("x",), gv_slots.at[turn], gv_part, gv_found)
+        gv_job = total_over(("x",), gv_slots.at[turn], fold(gram_of(items)), gv_found)
         next(gv_job)
-        if turn == 0:
-            next(gu_job)
         next(md_job)
         if turn == 0:
-            transpose_tiles(0, CAP // 2)
-            next(gu_job)
-            next(md_job)
-            transpose_tiles(CAP // 2, CAP)
+            transpose_tiles(0, CAP)
             drain(gu_job)
             gram_users = unfold(gu_found[0])
         drain(gv_job)
         gram_items = unfold(gv_found[0])
-        if turn:
-            next(md_job)
+        next(md_job)
         inv = inverse(gram_users * gram_items)
+        ahead = mm(inv, right_three(day_rows))
         drain(md_job)
         moments = md_found[0]
         square = moments * moments
         square = jnp.sum(jnp.sum(square, axis=1, keepdims=True), axis=0, keepdims=True)
         norm = jnp.sqrt(square / (R * DAYS) + EPSILON)
-        moments = moments / norm
         moments = jnp.concatenate(
             [moments[:, :DAYS]] + [pltpu.roll(moments, TILE - k * 32, 1)[:, :DAYS] for k in (1, 2, 3)], axis=0
         )
-        days = mm(inv, right_three(moments + day_rows))
+        days = mm(inv, right_three(moments)) * (1.0 / norm) + ahead
         for day in range(DAYS):
             spread[day] = jnp.broadcast_to(days[:, day : day + 1], (R, TILE))
         if final:
             day_out[...] = days.T
 
-        def user_product(tile, ub, ib, day):
-            return mm((items[ib] * spread[day]).astype(BF16), tile)
-
-        sweep(0, tiles_t, user_product)
+        def user_product(place, slot, ub, ib, day):
+            return mm((items[ib] * spread[day]).astype(BF16), tiles_t[slot])
+
+        sweep(0, user_product)
         assemble(0, mu)
         parts = [reduce_ring(mu, part, urecv.at[turn, part]) for part in range(2)]
         next(parts[0])
@@ -546,17 +563,22 @@
         gu_job = total_over(("core", "y", "z"), gu_slots.at[1 + turn], fold(gram_of(users)), gu_found)
         next(gu_job)
 
-        def item_product(tile, ub, ib, day):
-            return mm((users[ub] * spread[day]).astype(BF16), tile)
-
-        acc = sweep(1, tiles, item_product, 0, CAP // 2)
+        def item_product(place, slot, ub, ib, day):
+            return mm((users[ub] * spread[day]).astype(BF16), tiles[slot])
+
+        acc = sweep(1, item_product, 0, CAP // 2)
         next(gu_job)
-        sweep(1, tiles, item_product, CAP // 2, CAP, acc)
+        sweep(1, item_product, CAP // 2, CAP, acc)
         assemble(1, mi, 16 - core * 16, 16)
         job = reduce_plane(mi, irecv_core.at[turn], irecv.at[turn])
         next(job)
         assemble(1, mi, core * 16, 16)
         next(job)
+        if not final:
+            day_partials(0, CAP // 2)
+        next(gu_job)
+        if not final:
+            day_partials(CAP // 2, CAP)
         drain(gu_job)
         gram_users = unfold(gu_found[0])
         inv = inverse(gram_users * gram_days)
@@ -643,7 +665,7 @@
             pltpu.VMEM((PASSES, *block), F32),
             pltpu.VMEM((PASSES, *block), F32),
             pltpu.VMEM(block, F32),
-            pltpu.VMEM((1 + PASSES, 10, R // 2, 2 * R), F32),
+            pltpu.VMEM((1 + PASSES, 18, R // 2, 2 * R), F32),
             pltpu.VMEM((PASSES, 4, R // 2, 2 * R), F32),
             pltpu.VMEM((PASSES, 22, 16, TILE), F32),
             pltpu.VMEM((PASSES, 2, 22, 8, TILE), F32),

time: 152 us -> 148 us (0.974)
  Pallas kernels: 150 us -> 146 us
    pallas_call x1, Pallas kernels: 147 us -> 143 us  [shards(): pl.pallas_call(kernel, out_shape=(jax.ShapeDtypeStruct(user_prev.shape, F...]
where the time goes in v5:
time: 148 us
  Pallas kernels  146 us (99%)
    pallas_call x1, Pallas kernels, shards(): pl.pallas_call(kernel, out_shape=(jax.ShapeDtypeStruct(user_prev.shape, F...  143 us

profile of v5, /device:TPU:1, one launch (start us, length us, event | category | flops | bytes accessed | tf_op | source)
XLA Modules:
  0.0 147.6 jit_solution(8096509599967632322)
XLA Ops:
  1.3 143.4 %shard_map.85 = (f32[64,4096]{1,0:T(8,128)}, f32[64,4096]{1,0:T(8,128)}, f32[32,64]{1,0:T(8,128)}) custom-call(s32[3,256]{1,0:T(4,128)} %index.1, s32[1]{0:T(128)S(6)} %copy.9.live_count, bf16[256,128,128]{2,1,0:T(8,128)(2,1)} %tiles_hbm.1, f32[64,4096]{1,0:T(8,128)} %user_hbm.1, f32[64,4096]{1,0:T(8,128)} %item_hbm.1, f32[32,64]{1,0:T(8,128)} %bitcast.2), custom_call_target="tpu_custom_call" | custom-call | tf_op jit(solution)/shard_map/pallas_call | solution.py:643
  144.7 2.9 %shard_map.86 = (f32[64,4096]{1,0:T(8,128)}, f32[64,4096]{1,0:T(8,128)}, f32[32,64]{1,0:T(8,128)}) custom-call(f32[64,4096]{1,0:T(8,128)} %get-tuple-element.9.user_in, f32[64,4096]{1,0:T(8,128)} %get-tuple-element.10.item_in, f32[32,64]{1,0:T(8,128)} %get-tuple-element.11.day_in), custom_call_target="tpu_custom_call" | custom-call | tf_op jit(solution)/shard_map/pallas_call | solution.py:629

commit v6 on v5

--- a/solution.py
+++ b/solution.py
@@ -77,7 +77,7 @@
         return Group((self.send.at[self.used - 1], self.recv.at[self.used - 1]))
 
 
-GROUPS = 2 + PASSES * (3 + 1 + 3 + 3 + 3 + 4 + 4 + 4 + 1 + 4 + 1)
+GROUPS = 2 + PASSES * (3 + 1 + 3 + 3 + 3 + 4 + 4 + 4 + 1 + 15 + 1)
 
 
 def order_slots(index, live, codes, last):
@@ -272,16 +272,16 @@
     def gather_plane(source):
         own = core * 16
         here = source.at[own + plane]
-        flying = {row: groups.new() for row in range(4)}
-        for row in far_first:
-            for step in (row * 4 + further for further in far_first):
-                if step:
-                    flying[row].start(here, here, along_yz(step))
+        flying = {step: groups.new() for step in orders[16]}
+        for step in orders[16]:
+            flying[step].start(here, here, along_yz(step))
         yield
         between = groups.new()
-        for row in (0, 1, 3, 2):
-            flying[row].wait(source.at[pl.ds(0, 4 if row else 3)])
-            place = source.at[pl.ds(own + row_of(4 - row).start, 4)]
+        between.start(here, here, twin)
+        for step in reversed(orders[16]):
+            back = (4 - step // 4) % 4 * 4 + (4 - step % 4) % 4
+            place = source.at[own + plane_of(back)]
+            flying[step].wait(place)
             between.start(place, place, twin)
         yield
         between.wait(source.at[pl.ds(0, 16)])
@@ -365,17 +365,17 @@
         each_block(visit, 8, begin, count)
 
     def gram_of(source):
-        def four(step, carry):
+        def eight(step, carry):
             total, cross = carry
-            for k in range(2):
-                block = step * 4 + k * 2
+            for k in range(4):
+                block = step * 8 + k * 2
                 high, low = halves(jnp.concatenate([source[block], source[block + 1]], axis=1))
                 total = total + mm(high, high, NT)
                 cross = cross + mm(high, low, NT)
             return total, cross
 
         zero = jnp.zeros((R, R), F32)
-        total, cross = lax.fori_loop(0, BLOCKS // 4, four, (zero, zero))
+        total, cross = lax.fori_loop(0, BLOCKS // 8, eight, (zero, zero))
         return total + (cross + cross.T)
 
     def fold(gram):
@@ -420,7 +420,7 @@
             if out is not None:
                 out[:, columns(block)] = value
 
-        each_block(visit, 4, begin, count)
+        each_block(visit, 8, begin, count)
 
     order_slots(index, live_count[0], codes_made, last_made)
     codes_copy = pltpu.make_async_copy(codes_made, codes, order_sem.at[0])
@@ -478,13 +478,13 @@
             sweep(2, day_product)
 
         def day_sums(step, total):
-            for k in range(8):
-                day = step * 8 + k
+            for k in range(16):
+                day = step * 16 + k
                 value = jnp.sum(running[last[2, day]], axis=1, keepdims=True)
                 total = jnp.where(lanes == day, value, total)
             return total
 
-        moments = lax.fori_loop(0, DAYS // 8, day_sums, jnp.zeros((R, TILE), F32))
+        moments = lax.fori_loop(0, DAYS // 16, day_sums, jnp.zeros((R, TILE), F32))
         moments = (moments[:16] + pltpu.roll(moments[16:32], 32, 1)) + (
             pltpu.roll(moments[32:48], 64, 1) + pltpu.roll(moments[48:], 96, 1)
         )
@@ -614,24 +614,37 @@
         copy.wait()
 
 
-def copy_kernel(user_in, item_in, day_in, user_out, item_out, day_out, sem):
-    flying = [
-        pltpu.make_async_copy(source, target, sem.at[k])
-        for k, (source, target) in enumerate(((user_in, user_out), (item_in, item_out), (day_in, day_out)))
-    ]
-    for copy in flying:
+PIECES = 4
+
+
+def copy_kernel(user_in, item_in, day_in, user_out, item_out, day_out, user_held, item_held, day_held, sem):
+    jobs = [(day_in, day_held, day_out)]
+    for source, held, target in ((user_in, user_held, user_out), (item_in, item_held, item_out)):
+        size = R // PIECES
+        for k in range(PIECES):
+            rows = pl.ds(k * size, size)
+            jobs.append((source.at[rows], held.at[rows], target.at[rows]))
+    arriving = [pltpu.make_async_copy(one[0], one[1], sem.at[0, k]) for k, one in enumerate(jobs)]
+    leaving = [pltpu.make_async_copy(one[1], one[2], sem.at[1, k]) for k, one in enumerate(jobs)]
+    for copy in arriving:
         copy.start()
-    for copy in flying:
+    for copy, onward in zip(arriving, leaving):
         copy.wait()
+        onward.start()
+    for copy in leaving:
+        copy.wait()
 
 
 def copied(arrays):
+    anywhere = pl.BlockSpec(memory_space=pl.ANY)
     return pl.pallas_call(
         copy_kernel,
         out_shape=tuple(jax.ShapeDtypeStruct(one.shape, one.dtype) for one in arrays),
-        in_specs=[pl.BlockSpec(memory_space=pltpu.VMEM)] * 3,
-        out_specs=(pl.BlockSpec(memory_space=pl.ANY),) * 3,
-        scratch_shapes=[pltpu.SemaphoreType.DMA((3,))],
+        in_specs=[anywhere] * 3,
+        out_specs=(anywhere,) * 3,
+        scratch_shapes=[pltpu.VMEM(one.shape, one.dtype) for one in arrays]
+        + [pltpu.SemaphoreType.DMA((2, 1 + 2 * PIECES))],
+        compiler_params=pltpu.CompilerParams(vmem_limit_bytes=63 * 1024 * 1024),
     )(*arrays)
 
 

time: 148 us -> 146 us (0.986)
  Pallas kernels: 146 us -> 144 us
    pallas_call x1, Pallas kernels: 143 us -> 142 us  [shards(): pl.pallas_call(kernel, out_shape=(jax.ShapeDtypeStruct(user_prev.shape, F...]
where the time goes in v6:
time: 146 us; the launch traced here: 145 us
  Pallas kernels  144 us (99%)
    pallas_call x1, Pallas kernels, shards(): pl.pallas_call(kernel, out_shape=(jax.ShapeDtypeStruct(user_prev.shape, F...  142 us

profile of v6, /device:TPU:1, one launch (start us, length us, event | category | flops | bytes accessed | tf_op | source)
XLA Modules:
  0.0 145.4 jit_solution(15140520802611337588)
XLA Ops:
  1.3 141.7 %shard_map.85 = (f32[64,4096]{1,0:T(8,128)}, f32[64,4096]{1,0:T(8,128)}, f32[32,64]{1,0:T(8,128)}) custom-call(s32[3,256]{1,0:T(4,128)} %index.1, s32[1]{0:T(128)S(6)} %copy.9.live_count, bf16[256,128,128]{2,1,0:T(8,128)(2,1)} %tiles_hbm.1, f32[64,4096]{1,0:T(8,128)} %user_hbm.1, f32[64,4096]{1,0:T(8,128)} %item_hbm.1, f32[32,64]{1,0:T(8,128)} %bitcast.2), custom_call_target="tpu_custom_call" | custom-call | tf_op jit(solution)/shard_map/pallas_call | solution.py:656
  143.0 2.4 %shard_map.86 = (f32[64,4096]{1,0:T(8,128)}, f32[64,4096]{1,0:T(8,128)}, f32[32,64]{1,0:T(8,128)}) custom-call(f32[64,4096]{1,0:T(8,128)} %get-tuple-element.9.user_in, f32[64,4096]{1,0:T(8,128)} %get-tuple-element.10.item_in, f32[32,64]{1,0:T(8,128)} %get-tuple-element.11.day_in), custom_call_target="tpu_custom_call" | custom-call | tf_op jit(solution)/shard_map/pallas_call | solution.py:640

commit v7 on v6

--- a/solution.py
+++ b/solution.py
@@ -16,7 +16,7 @@
 EPSILON = 1e-06
 USER_ENTRIES = 64 * 131072
 ITEM_ENTRIES = 64 * 16384
-UNROLL = 64
+UNROLL = 128
 MESH = pl.DeviceIdType.MESH
 F32 = jnp.float32
 BF16 = jnp.bfloat16
@@ -77,7 +77,7 @@
         return Group((self.send.at[self.used - 1], self.recv.at[self.used - 1]))
 
 
-GROUPS = 2 + PASSES * (3 + 1 + 3 + 3 + 3 + 4 + 4 + 4 + 1 + 15 + 1)
+GROUPS = 2 + (3 + 1 + 3 + 3 + 3 + 4 + 4 + 4 + 1 + 15 + 1)
 
 
 def order_slots(index, live, codes, last):
@@ -456,6 +456,7 @@
     gu_job = total_over(("core", "yz"), gu_slots.at[0], gu_part, gu_found)
 
     for turn in range(PASSES):
+        groups.used = 0
         final = turn == PASSES - 1
 
         if turn == 0:
@@ -522,9 +523,11 @@
             return mm((items[ib] * spread[day]).astype(BF16), tiles_t[slot])
 
         sweep(0, user_product)
-        assemble(0, mu)
+        assemble(0, mu, lax.rem(x + 2, 4) * 8, 8)
         parts = [reduce_ring(mu, part, urecv.at[turn, part]) for part in range(2)]
         next(parts[0])
+        for share in (x + 1, x + 3, x):
+            assemble(0, mu, lax.rem(share, 4) * 8, 8)
         next(parts[0])
         next(parts[1])
         high, low = halves(days)
@@ -546,8 +549,8 @@
         )
         next(scale_job)
         next(scale_job)
+        next(jobs[0])
         prior_part(inv, user_prior)
-        next(jobs[0])
         next(jobs[1])
         next(scale_job)
         drain(scale_job)

time: 146 us -> 144 us (0.986)
  Pallas kernels: 144 us -> 142 us
    pallas_call x1, Pallas kernels: 142 us -> 139 us  [shards(): pl.pallas_call(kernel, out_shape=(jax.ShapeDtypeStruct(user_prev.shape, F...]
where the time goes in v7:
time: 144 us; the launch traced here: 143 us
  Pallas kernels  142 us (99%)
  between operations  1.45 us (1%)
    pallas_call x1, Pallas kernels, shards(): pl.pallas_call(kernel, out_shape=(jax.ShapeDtypeStruct(user_prev.shape, F...  139 us

profile of v7, /device:TPU:1, one launch (start us, length us, event | category | flops | bytes accessed | tf_op | source)
XLA Modules:
  0.0 143.3 jit_solution(6023070184064750484)
XLA Ops:
  1.3 139.5 %shard_map.85 = (f32[64,4096]{1,0:T(8,128)}, f32[64,4096]{1,0:T(8,128)}, f32[32,64]{1,0:T(8,128)}) custom-call(s32[3,256]{1,0:T(4,128)} %index.1, s32[1]{0:T(128)S(6)} %copy.9.live_count, bf16[256,128,128]{2,1,0:T(8,128)(2,1)} %tiles_hbm.1, f32[64,4096]{1,0:T(8,128)} %user_hbm.1, f32[64,4096]{1,0:T(8,128)} %item_hbm.1, f32[32,64]{1,0:T(8,128)} %bitcast.2), custom_call_target="tpu_custom_call" | custom-call | tf_op jit(solution)/shard_map/pallas_call | solution.py:659
  140.8 2.4 %shard_map.86 = (f32[64,4096]{1,0:T(8,128)}, f32[64,4096]{1,0:T(8,128)}, f32[32,64]{1,0:T(8,128)}) custom-call(f32[64,4096]{1,0:T(8,128)} %get-tuple-element.9.user_in, f32[64,4096]{1,0:T(8,128)} %get-tuple-element.10.item_in, f32[32,64]{1,0:T(8,128)} %get-tuple-element.11.day_in), custom_call_target="tpu_custom_call" | custom-call | tf_op jit(solution)/shard_map/pallas_call | solution.py:643
